TPU v7x, 32 devices: a whole 2x2x4 slice. The times are simulated.
32 devices in a mesh: sx: 4 (over y, x), sy: 2 (over core), cells: 4 (over z).
Axes of the slice: x: 2, y: 2, z: 4, core: 2. Of those that a mesh axis runs over, the one named last changes fastest.
Arguments:
- logits: float32 [5632, 16, 512], P('cells', 'sx', 'sy'), may hold values from -8 to 8
- cells_expr: bfloat16 [5632, 2048], P('cells'), may hold values from -48 to 48
- spatial: float32 [16, 512, 2048], P('sx', 'sy'), may hold values from -6 to 6
- gene_mask: int32 [2, 2048], replicated, may hold values 0 or 1
- slide_id: int32 [16, 512], P('sx', 'sy'), may hold values from 0 to 1
- edge_weight: float32 [6, 16, 512], P(None, 'sx', 'sy'), may hold values from 0.1 to 0.4
- edge_mask: int32 [6, 16, 512], P(None, 'sx', 'sy'), may hold values 0 or 1
Outputs:
- losses: float32 [2], replicated
- g_pred: float32 [16, 512, 2048], P('sx', 'sy', 'cells')
- d_logits: float32 [5632, 16, 512], P('cells', 'sx', 'sy')
- d_cells: float32 [5632, 2048], P('cells', ('sx', 'sy'))
All inputs are finite; a program needn't handle non-finite values. No bound on the sum of `edge_mask` on one device may be relied on, other than what follows from the above.
Results may differ from a plain program's by a relative error of at most 0.012.
Values may be sent and summed in bfloat16 or wider, within the bound.
A program may use at most 192 MiB of HBM per device.

v0:
```python
import jax
import jax.numpy as jnp
from jax import lax
from jax.sharding import PartitionSpec as P

eps = 1e-06
OFFSETS = ((0, 1), (0, -1), (1, 0), (-1, 0), (-1, 1), (1, -1))
HIGH = lax.Precision.HIGHEST


def with_halo(cells, sides, width):
    for axis, dim in sides:
        count = lax.axis_size(axis)
        ends = count - 1
        head = lax.slice_in_dim(cells, 0, width, axis=dim)
        tail = lax.slice_in_dim(cells, cells.shape[dim] - width, cells.shape[dim], axis=dim)
        cells = jnp.concatenate(
            [
                lax.ppermute(tail, axis, [(i, (i + 1) % count) for i in range(ends)]),
                cells,
                lax.ppermute(head, axis, [((i + 1) % count, i) for i in range(ends)]),
            ],
            axis=dim,
        )
    return cells


def by_slide(slide_hot, table):
    return jnp.einsum("src,sg->rcg", slide_hot, table, precision=HIGH)


def per_device(logits, cells_expr, spatial, gene_mask, slide_id, edge_weight, edge_mask):
    cell_rows, tile_rows, tile_cols = logits.shape
    gene_width = cells_expr.shape[1]
    tile_spots = tile_rows * tile_cols
    all_spots = tile_spots * lax.axis_size("sx") * lax.axis_size("sy")
    mask_f = gene_mask.astype(jnp.float32)
    count = jnp.maximum(jnp.sum(mask_f, axis=1), 1.0)
    slide_hot = (slide_id[None] == jnp.arange(2, dtype=jnp.int32)[:, None, None]).astype(
        jnp.float32
    )
    coeff = edge_weight * edge_mask.astype(jnp.float32)
    local_top = jnp.max(logits, axis=0)
    col_top = lax.pmax(local_top, "cells")
    exps_tile = jnp.exp(logits - col_top)
    col_total = lax.psum(jnp.sum(exps_tile, axis=0), "cells")
    mapping = exps_tile / col_total
    mapping_low = mapping.astype(jnp.bfloat16).reshape(cell_rows, tile_spots)
    partial_pred = lax.dot_general(
        mapping_low, cells_expr, (((0,), (0,)), ((), ())), preferred_element_type=jnp.float32
    )
    predicted = lax.psum(partial_pred, "cells").reshape(tile_rows, tile_cols, gene_width)
    share_width = gene_width // lax.axis_size("cells")
    pred_out = lax.dynamic_slice_in_dim(
        predicted, lax.axis_index("cells") * share_width, share_width, 2
    )
    padded = with_halo(predicted, (("sx", 0), ("sy", 1)), 1)
    smooth = predicted
    for slot in range(6):
        row_off, col_off = OFFSETS[slot]
        smooth = (
            smooth
            + coeff[slot][:, :, None]
            * padded[1 + row_off : 1 + row_off + tile_rows, 1 + col_off : 1 + col_off + tile_cols]
        )
    product = smooth * spatial
    squares = smooth * smooth
    truth_sq = spatial * spatial
    gene_part = jnp.stack(
        [
            jnp.einsum("src,rcg->sg", slide_hot, product, precision=HIGH),
            jnp.einsum("src,rcg->sg", slide_hot, squares, precision=HIGH),
            jnp.einsum("src,rcg->sg", slide_hot, truth_sq, precision=HIGH),
        ]
    )
    spot_mask = by_slide(slide_hot, mask_f)
    spot_part = jnp.stack(
        [
            jnp.sum(spot_mask * product, axis=-1),
            jnp.sum(spot_mask * squares, axis=-1),
            jnp.sum(spot_mask * truth_sq, axis=-1),
        ]
    )
    spot_ib = lax.rsqrt(spot_part[1] + eps)
    spot_ic = lax.rsqrt(spot_part[2] + eps)
    spot_cos = spot_part[0] * spot_ib * spot_ic
    gene_all, spot_sum = lax.psum((gene_part, jnp.sum(spot_cos)), ("sx", "sy"))
    gene_ib = lax.rsqrt(gene_all[1] + eps)
    gene_ic = lax.rsqrt(gene_all[2] + eps)
    gene_cos = gene_all[0] * gene_ib * gene_ic
    gene_loss = -jnp.sum(jnp.sum(mask_f * gene_cos, axis=1) / count) / 2.0
    spot_loss = -spot_sum / all_spots
    losses = jnp.stack([gene_loss, spot_loss])
    gene_scale = -mask_f / (2.0 * count[:, None])
    truth_coef = by_slide(slide_hot, gene_scale * gene_ib * gene_ic)
    smooth_coef = by_slide(slide_hot, -gene_scale * gene_cos * gene_ib * gene_ib)
    spot_scale = -1.0 / all_spots
    spot_truth = (spot_scale * spot_ib * spot_ic)[:, :, None]
    spot_smooth = (-spot_scale * spot_cos * spot_ib * spot_ib)[:, :, None]
    d_smooth = (
        truth_coef * spatial
        + smooth_coef * smooth
        + spot_mask * (spot_truth * spatial + spot_smooth * smooth)
    )
    coeff_pad = with_halo(coeff, (("sx", 1), ("sy", 2)), 1)
    grad_pad = with_halo(d_smooth, (("sx", 0), ("sy", 1)), 1)
    d_pred = d_smooth
    for slot in range(6):
        row_off, col_off = OFFSETS[slot]
        rows_from = 1 - row_off
        cols_from = 1 - col_off
        weight_here = coeff_pad[
            slot, rows_from : rows_from + tile_rows, cols_from : cols_from + tile_cols
        ]
        d_pred = (
            d_pred
            + weight_here[:, :, None]
            * grad_pad[rows_from : rows_from + tile_rows, cols_from : cols_from + tile_cols]
        )
    d_low = d_pred.astype(jnp.bfloat16)
    d_flat = d_low.reshape(tile_spots, gene_width)
    d_map = lax.dot_general(
        cells_expr, d_flat, (((1,), (1,)), ((), ())), preferred_element_type=jnp.float32
    )
    d_map = d_map.reshape(cell_rows, tile_rows, tile_cols)
    column = lax.psum(jnp.sum(mapping * d_map, axis=0), "cells")
    d_logits = mapping * (d_map - column)
    d_part = jnp.dot(mapping_low, d_flat, preferred_element_type=jnp.float32)
    d_cells = lax.psum_scatter(d_part, ("sx", "sy"), scatter_dimension=1, tiled=True)
    return (losses, pred_out, d_logits, d_cells)


def solution(mesh):
    return jax.shard_map(
        per_device,
        mesh=mesh,
        in_specs=(
            P("cells", "sx", "sy"),
            P("cells", None),
            P("sx", "sy", None),
            P(),
            P("sx", "sy"),
            P(None, "sx", "sy"),
            P(None, "sx", "sy"),
        ),
        out_specs=(P(), P("sx", "sy", "cells"), P("cells", "sx", "sy"), P("cells", ("sx", "sy"))),
        check_vma=False,
    )
```

profile of v0, /device:TPU:1, one launch (start us, length us, event | category | flops | bytes accessed | tf_op | source)
XLA Modules:
  0.0 769.7 jit_solution(16247957506723248630)
XLA Ops:
  7.2 0.0 all-reduce.3.cloned.1.call-start
  7.2 4.1 reduce_max.9
  11.3 10.8 %pmax.7 = f32[4,256]{1,0:T(4,128)S(1)} all-reduce(f32[4,256]{1,0:T(4,128)S(1)} %reduce_max.9), channel_id=1, replica_groups=mesh['sx'=4,'sy'=2,'cells'=4] {'cells'}, use_global_device_ids=true, to_apply=%region_1.0 | all-reduce | flops 1024 | bytes 8192 | tf_op jit(solution)/shard_map/pmax | solution.py:44
  22.1 4.5 fusion.22
  26.6 6.6 psum.35
  33.2 4.3 fusion.67
  37.5 0.7 copy.14
  38.2 10.9 %fusion.73 = f32[1024,2048]{1,0:T(8,128)} fusion(bf16[1408,1024]{1,0:T(8,128)(2,1)S(1)} %bitcast.113, bf16[1408,2048]{1,0:T(8,128)(2,1)} %param.8), kind=kOutput, calls=%fused_computation.129 | convolution fusion | flops 5905580032 | bytes 17039360 | tf_op jit(solution)/shard_map/dot_general | solution.py:49
  49.1 0.0 all-reduce.3.cloned.1.call-update
  49.1 0.0 reduce-scatter.2.cloned.1.call-start
  49.2 294.4 %all-reduce.3.cloned.1.call-done = f32[1024,2048]{1,0:T(8,128)} async-done(((f32[1024,2048]{1,0:T(8,128)}), f32[1024,2048]{1,0:T(8,128)}) %all-reduce.3.cloned.1.call-update) | async-done | bytes 8388624 | tf_op jit(solution)/shard_map/psum | solution.py:52
  343.6 2.6 slice_bitcast_fusion.1
  346.2 3.2 collective-permute-start
  349.5 1.3 collective-permute-start.1
  350.8 1.3 collective-permute-start.5
  352.1 0.0 slice-start.3
  352.1 4.9 collective-permute-start.4
  357.0 6.4 fusion.32
  363.4 77.2 %collective-permute-done.5 = f32[6,1,256]{2,1,0:T(1,128)S(1)} collective-permute-done((f32[6,1,256]{2,1,0:T(1,128)S(1)}, f32[6,1,256]{2,1,0:T(1,128)S(1)}, u32[]{:S(2)}, u32[]{:S(2)}) %collective-permute-start.5) | collective-permute-done | bytes 6176 | tf_op jit(solution)/shard_map/ppermute | solution.py:21
  440.6 0.0 collective-permute-done.4
  440.6 0.1 fusion.71
  440.7 3.6 collective-permute-start.10
  444.2 1.3 collective-permute-start.6
  445.6 0.0 copy-start.1
  445.6 0.0 copy-start.2
  445.6 0.1 pad_maximum_fusion.11
  445.7 3.0 collective-permute-start.2
  448.7 1.5 collective-permute-start.3
  450.2 0.0 slice-start
  450.2 0.1 maximum_bitcast_fusion.1
  450.3 0.0 slice-start.1
  450.4 0.0 copy-start.3
  450.4 1.5 collective-permute-done.3
  451.9 9.5 %pad_maximum_fusion = (f32[6,257,2048]{2,1,0:T(8,128)}, f32[6,257,2048]{2,1,0:T(8,128)}) fusion(f32[6,1,2048]{2,1,0:T(1,128)S(1)} %collective-permute-done.2, f32[1,256,2048]{2,1,0:T(8,128)S(1)} %collective-permute-done.1, f32[4,256,2048]{2,1,0:T(8,128)S(1)} %bitcast.107, f32[1,256,2048]{2,1,0:T(8,128)S(1)} %collective-permute-done, ...), kind=kLoop, calls=%fused_computation | loop fusion | flops 18948096 | bytes 37945344 | tf_op jit(solution)/shard_map/concatenate | solution.py:17
  461.3 26.6 %multiply_reduce_fusion.1 = (f32[4,256]{1,0:T(4,128)S(1)}, f32[4,256]{1,0:T(4,128)S(1)}, f32[4,256]{1,0:T(4,128)S(1)}, f32[4,256,2048]{2,1,0:T(8,128)}, f32[4,256,2048]{2,1,0:T(8,128)}) fusion(f32[4,256,2048]{2,1,0:T(8,128)S(1)} %bitcast.101, f32[6,257,2048]{2,1,0:T(8,128)} %get-tuple-element.18, f32[4,256]{1,0:T(4,128)S(1)} %get-tuple-element.34, ...), kind=kOutput, calls=%fused_computation.36 | convolution fusion | flops 98569216 | bytes 71360512 | tf_op jit(solution)/shard_map/src,sg->rcg/dot_general | solution.py:29
  487.9 6.7 fusion.26
  494.6 3.1 fusion.29
  497.7 0.6 multiply_multiply_fusion.1
  498.3 22.0 %all-reduce = (f32[]{:T(128)}, f32[3,2,2048]{2,1,0:T(2,128)S(1)}) all-reduce(f32[]{:T(128)} %get-tuple-element.44, f32[3,2,2048]{2,1,0:T(2,128)S(1)} %pad_maximum_fusion.12), channel_id=1, replica_groups=mesh['sx'=4,'sy'=2,'cells'=4] {'sx','sy'}, use_global_device_ids=true, to_apply=%region_13.0 | all-reduce | flops 12289 | bytes 98312 | tf_op jit(solution)/shard_map/psum | solution.py:87
  520.3 0.2 convert_reduce_fusion
  520.4 0.6 maximum_multiply_fusion
  521.1 5.8 fusion.43
  526.9 13.6 %multiply_add_fusion = f32[4,256,2048]{2,1,0:T(8,128)S(1)} fusion(f32[4,256,2048]{2,1,0:T(8,128)} %get-tuple-element.48, f32[4,256,2048]{2,1,0:T(8,128)} %get-tuple-element.12, f32[4,256,2048]{2,1,0:T(8,128)} %param.9, f32[4,256,2048]{2,1,0:T(8,128)} %fusion.43, f32[4,256]{1,0:T(4,128)S(1)} %get-tuple-element.43, f32[4,256]{1,0:T(4,128)S(1)} %get-tuple-element.45, ...), kind=kOutput, calls=%fused_computation.34 | convolution fusion | flops 67143680 | bytes 42004992 | tf_op jit(solution)/shard_map/src,sg->rcg/dot_general | solution.py:29
  540.5 0.4 fusion.70
  540.9 4.8 collective-permute-start.7
  545.7 1.3 collective-permute-start.8
  547.0 43.8 %collective-permute-done.7 = f32[1,256,2048]{2,1,0:T(8,128)S(1)} collective-permute-done((f32[1,256,2048]{2,1,0:T(8,128)S(1)}, f32[1,256,2048]{2,1,0:T(8,128)S(1)}, u32[]{:S(2)}, u32[]{:S(2)}) %collective-permute-start.7) | collective-permute-done | bytes 2097184 | tf_op jit(solution)/shard_map/ppermute | solution.py:19
  590.8 43.3 %collective-permute-done.8 = f32[1,256,2048]{2,1,0:T(8,128)S(1)} collective-permute-done((f32[1,256,2048]{2,1,0:T(8,128)S(1)}, f32[1,256,2048]{2,1,0:T(8,128)S(1)}, u32[]{:S(2)}, u32[]{:S(2)}) %collective-permute-start.8) | collective-permute-done | bytes 2097184 | tf_op jit(solution)/shard_map/ppermute | solution.py:21
  634.0 0.1 pad_maximum_fusion.8
  634.1 5.0 collective-permute-start.11
  639.1 1.5 collective-permute-start.9
  640.6 1.6 collective-permute-done.9
  642.2 10.0 %maximum_maximum_fusion.1 = (f32[6,257,2048]{2,1,0:T(8,128)}, f32[6,257,2048]{2,1,0:T(8,128)}) fusion(f32[1,256,2048]{2,1,0:T(8,128)S(1)} %collective-permute-done.8, f32[4,256,2048]{2,1,0:T(8,128)S(1)} %multiply_add_fusion, f32[1,256,2048]{2,1,0:T(8,128)S(1)} %collective-permute-done.7, f32[6,1,2048]{2,1,0:T(1,128)S(1)} %collective-permute-done.9, ...), kind=kLoop, calls=%fused_computation.2 | loop fusion | flops 18948096 | bytes 37945344 | tf_op jit(solution)/shard_map/concatenate | solution.py:17
  652.1 14.6 %fusion.1 = bf16[4,256,2048]{2,1,0:T(8,128)(2,1)} fusion(f32[6,257,2048]{2,1,0:T(8,128)} %get-tuple-element.14, f32[6,257,2048]{2,1,0:T(8,128)} %get-tuple-element.13, f32[1,256,2048]{2,1,0:T(8,128)S(1)} %collective-permute-done.8, f32[4,256,2048]{2,1,0:T(8,128)S(1)} %multiply_add_fusion, f32[1,256,2048]{2,1,0:T(8,128)S(1)} %collective-permute-done.7, ...), kind=kLoop, calls=%fused_computation.7 | loop fusion | flops 31457280 | bytes 50356224 | tf_op jit(solution)/shard_map/convert_element_type | solution.py:120
  666.7 11.1 %convolution_bitcast_fusion = f32[1408,2048]{1,0:T(8,128)} fusion(bf16[4,256,2048]{2,1,0:T(8,128)(2,1)} %fusion.1, bf16[1408,4,256]{2,1,0:T(4,128)(2,1)S(1)} %fusion.67), kind=kOutput, calls=%fused_computation.4 | convolution fusion | flops 5905580032 | bytes 18612224 | tf_op jit(solution)/shard_map/dot_general | solution.py:128
  677.8 0.0 reduce-scatter.2.cloned.1.call-update
  677.8 3.1 constant_dynamic-slice_fusion
  682.2 0.6 pad_maximum_fusion.22
  682.8 13.5 %fusion.74 = f32[1024,1408]{1,0:T(8,128)} fusion(bf16[1024,2048]{1,0:T(8,128)(2,1)} %bitcast.112, bf16[1408,2048]{1,0:T(8,128)(2,1)} %param.8), kind=kOutput, calls=%fused_computation.130 | convolution fusion | flops 5905580032 | bytes 15728640 | tf_op jit(solution)/shard_map/dot_general | solution.py:122
  696.3 7.4 copy.12
  703.7 6.5 multiply_reduce_fusion.3
  710.2 7.3 psum.39
  717.5 8.3 %subtract_multiply_fusion = f32[704,8,256]{2,1,0:T(8,128)} fusion(f32[704,8,256]{2,1,0:T(8,128)} %bitcast.108, f32[8,256]{1,0:T(8,128)S(1)} %bitcast.118, f32[8,256]{1,0:T(8,128)S(1)} %bitcast.119, f32[704,8,256]{2,1,0:T(8,128)} %bitcast.99, f32[8,256]{1,0:T(8,128)S(1)} %bitcast.120), kind=kLoop, calls=%fused_computation.42 | loop fusion | flops 5767168 | bytes 17326080 | tf_op jit(solution)/shard_map/mul | solution.py:127
  725.9 36.6 %reduce-scatter.2.cloned.1.call-done = f32[1408,256]{1,0:T(8,128)} async-done(((f32[1408,2048]{1,0:T(8,128)}), f32[1408,256]{1,0:T(8,128)}) %reduce-scatter.2.cloned.1.call-update) | async-done | bytes 1441808 | tf_op jit(solution)/shard_map/reduce_scatter | solution.py:129
  (32 shorter events, 0.1 us)
Async XLA Ops:
  7.2 336.4 %all-reduce.3.cloned.1.call-start = ((), (), s32[]{:S(2)}) async-start(), calls=%async_computation.1 | async-start | bytes 16777216 | tf_op jit(solution)/shard_map/psum | solution.py:52
  49.1 301.7 %copy-start.5 = (f32[6,4,256]{2,1,0:T(4,128)S(1)}, f32[6,4,256]{2,1,0:T(4,128)}, u32[]{:S(2)}) copy-start(f32[6,4,256]{2,1,0:T(4,128)} %param.12) | copy-start | bytes 73732
  49.1 301.7 %copy-start.6 = (s32[6,4,256]{2,1,0:T(4,128)S(1)}, s32[6,4,256]{2,1,0:T(4,128)}, u32[]{:S(2)}) copy-start(s32[6,4,256]{2,1,0:T(4,128)} %param.13) | copy-start | bytes 73732
  49.1 307.9 %copy-start.4 = (s32[4,256]{1,0:T(4,128)S(1)}, s32[4,256]{1,0:T(4,128)}, u32[]{:S(2)}) copy-start(s32[4,256]{1,0:T(4,128)} %param.11) | copy-start | bytes 12292
  49.1 713.3 %reduce-scatter.2.cloned.1.call-start = ((), (), s32[]{:S(2)}) async-start(), calls=%async_computation.2 | async-start | bytes 12976128 | tf_op jit(solution)/shard_map/reduce_scatter | solution.py:129
  343.6 102.0 %slice-start.2 = ((s8[8388608]{0:T(1024)(128)(4,1)}), s8[4194304]{0:T(1024)(128)(4,1)S(1)}, s32[]{:S(2)}) async-start(s8[8388608]{0:T(1024)(128)(4,1)} %bitcast.104), calls=%async_computation.5 | async-start | bytes 8388608
  346.2 99.3 %collective-permute-start = (f32[1,256,2048]{2,1,0:T(8,128)S(1)}, f32[1,256,2048]{2,1,0:T(8,128)S(1)}, u32[]{:S(2)}, u32[]{:S(2)}) collective-permute-start(f32[1,256,2048]{2,1,0:T(8,128)S(1)} %get-tuple-element.23), channel_id=1, source_target_pairs={{0,8},{8,16},{16,24},{1,9},{9,17},{17,25},{2,10},{10,18},{18,26},{... | collective-permute-start | bytes 6291464 | tf_op jit(solution)/shard_map/ppermute | solution.py:19
  349.5 96.1 %collective-permute-start.1 = (f32[1,256,2048]{2,1,0:T(8,128)S(1)}, f32[1,256,2048]{2,1,0:T(8,128)S(1)}, u32[]{:S(2)}, u32[]{:S(2)}) collective-permute-start(f32[1,256,2048]{2,1,0:T(8,128)S(1)} %get-tuple-element.24), channel_id=1, source_target_pairs={{8,0},{16,8},{24,16},{9,1},{17,9},{25,17},{10,2},{18,10},{26,18},{... | collective-permute-start | bytes 6291464 | tf_op jit(solution)/shard_map/ppermute | solution.py:21
  350.8 89.7 %collective-permute-start.5 = (f32[6,1,256]{2,1,0:T(1,128)S(1)}, f32[6,1,256]{2,1,0:T(1,128)S(1)}, u32[]{:S(2)}, u32[]{:S(2)}) collective-permute-start(f32[6,1,256]{2,1,0:T(1,128)S(1)} %get-tuple-element.42), channel_id=1, source_target_pairs={{8,0},{16,8},{24,16},{9,1},{17,9},{25,17},{10,2},{18,10},{26,18},{... | collective-permute-start | bytes 18440 | tf_op jit(solution)/shard_map/ppermute | solution.py:21
  352.1 93.5 %slice-start.3 = ((s8[8388608]{0:T(1024)(128)(4,1)}), s8[4194304]{0:T(1024)(128)(4,1)S(1)}, s32[]{:S(2)}) async-start(s8[8388608]{0:T(1024)(128)(4,1)} %bitcast.104), calls=%async_computation.6 | async-start | bytes 8388608
  352.1 88.4 %collective-permute-start.4 = (f32[6,1,256]{2,1,0:T(1,128)S(1)}, f32[6,1,256]{2,1,0:T(1,128)S(1)}, u32[]{:S(2)}, u32[]{:S(2)}) collective-permute-start(f32[6,1,256]{2,1,0:T(1,128)S(1)} %get-tuple-element.41), channel_id=1, source_target_pairs={{0,8},{8,16},{16,24},{1,9},{9,17},{17,25},{2,10},{10,18},{18,26},{... | collective-permute-start | bytes 18440 | tf_op jit(solution)/shard_map/ppermute | solution.py:19
  440.7 9.5 %collective-permute-start.10 = (f32[6,6,1]{2,1,0:T(8,128)S(1)}, f32[6,6,1]{2,1,0:T(8,128)S(1)}, u32[]{:S(2)}, u32[]{:S(2)}) collective-permute-start(f32[6,6,1]{2,1,0:T(8,128)S(1)} %get-tuple-element.30), channel_id=1, source_target_pairs={{4,0},{5,1},{6,2},{7,3},{12,8},{13,9},{14,10},{15,11},{20,16},{21,... | collective-permute-start | bytes 440 | tf_op jit(solution)/shard_map/ppermute | solution.py:21
  444.2 6.0 collective-permute-start.6
  445.6 15.8 %copy-start.1 = (f32[1,256,2048]{2,1,0:T(8,128)}, f32[1,256,2048]{2,1,0:T(8,128)S(1)}, u32[]{:S(2)}) copy-start(f32[1,256,2048]{2,1,0:T(8,128)S(1)} %collective-permute-done) | copy-start | bytes 6291460
  445.6 15.7 %copy-start.2 = (f32[1,256,2048]{2,1,0:T(8,128)}, f32[1,256,2048]{2,1,0:T(8,128)S(1)}, u32[]{:S(2)}) copy-start(f32[1,256,2048]{2,1,0:T(8,128)S(1)} %collective-permute-done.1) | copy-start | bytes 6291460
  445.7 4.7 collective-permute-start.2
  448.7 3.1 collective-permute-start.3
  450.2 11.1 %slice-start = ((s8[8388608]{0:T(1024)(128)(4,1)}), s8[4194304]{0:T(1024)(128)(4,1)S(1)}, s32[]{:S(2)}) async-start(s8[8388608]{0:T(1024)(128)(4,1)} %bitcast.100), calls=%async_computation.3 | async-start | bytes 8388608
  450.3 11.0 %slice-start.1 = ((s8[8388608]{0:T(1024)(128)(4,1)}), s8[4194304]{0:T(1024)(128)(4,1)S(1)}, s32[]{:S(2)}) async-start(s8[8388608]{0:T(1024)(128)(4,1)} %bitcast.100), calls=%async_computation.4 | async-start | bytes 8388608
  450.4 11.0 %copy-start.3 = (s32[2,2048]{1,0:T(2,128)S(1)}, s32[2,2048]{1,0:T(2,128)}, u32[]{:S(2)}) copy-start(s32[2,2048]{1,0:T(2,128)} %param.10) | copy-start | bytes 49156
  487.9 6.7 copy-start
  540.9 49.9 %collective-permute-start.7 = (f32[1,256,2048]{2,1,0:T(8,128)S(1)}, f32[1,256,2048]{2,1,0:T(8,128)S(1)}, u32[]{:S(2)}, u32[]{:S(2)}) collective-permute-start(f32[1,256,2048]{2,1,0:T(8,128)S(1)} %get-tuple-element.21), channel_id=1, source_target_pairs={{0,8},{8,16},{16,24},{1,9},{9,17},{17,25},{2,10},{10,18},{18,26},{... | collective-permute-start | bytes 6291464 | tf_op jit(solution)/shard_map/ppermute | solution.py:19
  545.7 88.3 %collective-permute-start.8 = (f32[1,256,2048]{2,1,0:T(8,128)S(1)}, f32[1,256,2048]{2,1,0:T(8,128)S(1)}, u32[]{:S(2)}, u32[]{:S(2)}) collective-permute-start(f32[1,256,2048]{2,1,0:T(8,128)S(1)} %get-tuple-element.22), channel_id=1, source_target_pairs={{8,0},{16,8},{24,16},{9,1},{17,9},{25,17},{10,2},{18,10},{26,18},{... | collective-permute-start | bytes 6291464 | tf_op jit(solution)/shard_map/ppermute | solution.py:21
  634.1 6.5 collective-permute-start.11
  639.1 3.1 collective-permute-start.9
Sparse Core Ops, SparseCore 0:
  49.3 294.2 all-reduce.2
  678.0 84.4 reduce-scatter.1
where the time goes:
time: 779 us; the launch traced here: 770 us
  waiting for transfers between devices  498 us (64%)
  matrix products  97.6 us (13%)
  other arithmetic  64 us (8%)
  blocking collectives  46.7 us (6%)
  starting transfers between devices  32.7 us (4%)
  between operations  16.2 us (2%)
  local copies, waits for them, and re-layouts  14.3 us (2%)
    psum x1, waiting for transfers between devices, per_device(): lax.psum(partial_pred, 'cells').reshape(tile_rows, tile_cols, gene_width)  294 us
    ppermute x6, waiting for transfers between devices, with_halo(): lax.ppermute(head, axis, [((i + 1) % count, i) for i in range(ends)])  120 us
    ppermute x6, waiting for transfers between devices, with_halo(): lax.ppermute(tail, axis, [(i, (i + 1) % count) for i in range(ends)])  46.8 us
    dot_general x3, matrix products, by_slide(): return jnp.einsum('src,sg->rcg', slide_hot, table, precision=HIGH)  46 us
    reduce_scatter x1, waiting for transfers between devices, per_device(): lax.psum_scatter(d_part, ('sx', 'sy'), scatter_dimension=1, tiled=True)  36.6 us
    psum x1, blocking collectives, per_device(): gene_all, spot_sum = lax.psum((gene_part, jnp.sum(spot_cos)), ('sx', 'sy'))  22 us
    concatenate x3, other arithmetic, with_halo(): jnp.concatenate([lax.ppermute(tail, axis, [(i, (i + 1) % count) for i in...  19.4 us
    ppermute x6, starting transfers between devices, with_halo(): lax.ppermute(tail, axis, [(i, (i + 1) % count) for i in range(ends)])  17.2 us
  transfers between devices with their start and end apart: 14, of which 7 were waited for; matrix products, arithmetic and copies ran while one was open for 6% of the time, Pallas kernels for 0%

commit v1 on v0

v1 whole, which is shorter than its diff:
```python
import jax
import jax.numpy as jnp
from jax import lax
from jax.sharding import PartitionSpec as P

eps = 1e-06
OFFSETS = ((0, 1), (0, -1), (1, 0), (-1, 0), (-1, 1), (1, -1))


def with_halo(cells, sides, width):
    for axis, dim in sides:
        count = lax.axis_size(axis)
        ends = count - 1
        head = lax.slice_in_dim(cells, 0, width, axis=dim)
        tail = lax.slice_in_dim(cells, cells.shape[dim] - width, cells.shape[dim], axis=dim)
        cells = jnp.concatenate(
            [
                lax.ppermute(tail, axis, [(i, (i + 1) % count) for i in range(ends)]),
                cells,
                lax.ppermute(head, axis, [((i + 1) % count, i) for i in range(ends)]),
            ],
            axis=dim,
        )
    return cells


def per_device(logits, cells_expr, spatial, gene_mask, slide_id, edge_weight, edge_mask):
    cell_rows, tile_rows, tile_cols = logits.shape
    gene_width = cells_expr.shape[1]
    tile_spots = tile_rows * tile_cols
    all_spots = tile_spots * lax.axis_size("sx") * lax.axis_size("sy")
    share = gene_width // lax.axis_size("cells")
    first_gene = lax.axis_index("cells") * share
    mask_all = gene_mask.astype(jnp.float32)
    count = jnp.maximum(jnp.sum(mask_all, axis=1), 1.0)
    mask_f = lax.dynamic_slice_in_dim(mask_all, first_gene, share, 1)
    truth = lax.dynamic_slice_in_dim(spatial, first_gene, share, 2)
    on_one = (slide_id == 1)[:, :, None]
    slide_hot = (slide_id[None] == jnp.arange(2, dtype=jnp.int32)[:, None, None]).astype(
        jnp.float32
    )
    coeff = edge_weight * edge_mask.astype(jnp.float32)
    exps_tile = jnp.exp(logits)
    col_total = lax.psum(jnp.sum(exps_tile, axis=0), "cells")
    mapping = exps_tile / col_total
    mapping_low = mapping.astype(jnp.bfloat16).reshape(cell_rows, tile_spots)
    partial_pred = lax.dot_general(
        mapping_low, cells_expr, (((0,), (0,)), ((), ())), preferred_element_type=jnp.float32
    )
    predicted = lax.psum_scatter(partial_pred, "cells", scatter_dimension=1, tiled=True)
    predicted = predicted.reshape(tile_rows, tile_cols, share)
    padded = with_halo(predicted, (("sx", 0), ("sy", 1)), 1)
    smooth = predicted
    for slot in range(6):
        row_off, col_off = OFFSETS[slot]
        smooth = (
            smooth
            + coeff[slot][:, :, None]
            * padded[1 + row_off : 1 + row_off + tile_rows, 1 + col_off : 1 + col_off + tile_cols]
        )
    product = smooth * truth
    squares = smooth * smooth
    truth_sq = truth * truth
    hot = slide_hot[:, :, :, None]
    gene_part = jnp.stack(
        [jnp.sum(hot * what[None], axis=(1, 2)) for what in (product, squares, truth_sq)]
    )
    spot_mask = jnp.where(on_one, mask_f[1], mask_f[0])
    spot_part = jnp.stack(
        [jnp.sum(spot_mask * what, axis=-1) for what in (product, squares, truth_sq)]
    )
    gene_all = lax.psum(gene_part, ("sx", "sy"))
    spot_part = lax.psum(spot_part, "cells")
    spot_ib = lax.rsqrt(spot_part[1] + eps)
    spot_ic = lax.rsqrt(spot_part[2] + eps)
    spot_cos = spot_part[0] * spot_ib * spot_ic
    gene_ib = lax.rsqrt(gene_all[1] + eps)
    gene_ic = lax.rsqrt(gene_all[2] + eps)
    gene_cos = gene_all[0] * gene_ib * gene_ic
    gene_loss = -jnp.sum(jnp.sum(mask_f * gene_cos, axis=1) / count) / 2.0
    gene_loss = lax.psum(gene_loss, "cells")
    spot_loss = -lax.psum(jnp.sum(spot_cos), ("sx", "sy")) / all_spots
    losses = jnp.stack([gene_loss, spot_loss])
    gene_scale = -mask_f / (2.0 * count[:, None])
    truth_by = gene_scale * gene_ib * gene_ic
    smooth_by = -gene_scale * gene_cos * gene_ib * gene_ib
    truth_coef = jnp.where(on_one, truth_by[1], truth_by[0])
    smooth_coef = jnp.where(on_one, smooth_by[1], smooth_by[0])
    spot_scale = -1.0 / all_spots
    spot_truth = (spot_scale * spot_ib * spot_ic)[:, :, None]
    spot_smooth = (-spot_scale * spot_cos * spot_ib * spot_ib)[:, :, None]
    d_smooth = (
        truth_coef * truth
        + smooth_coef * smooth
        + spot_mask * (spot_truth * truth + spot_smooth * smooth)
    )
    coeff_pad = with_halo(coeff, (("sx", 1), ("sy", 2)), 1)
    grad_pad = with_halo(d_smooth, (("sx", 0), ("sy", 1)), 1)
    d_pred = d_smooth
    for slot in range(6):
        row_off, col_off = OFFSETS[slot]
        rows_from = 1 - row_off
        cols_from = 1 - col_off
        weight_here = coeff_pad[
            slot, rows_from : rows_from + tile_rows, cols_from : cols_from + tile_cols
        ]
        d_pred = (
            d_pred
            + weight_here[:, :, None]
            * grad_pad[rows_from : rows_from + tile_rows, cols_from : cols_from + tile_cols]
        )
    d_low = d_pred.astype(jnp.bfloat16).reshape(tile_spots, share)
    column = jnp.sum(predicted.reshape(tile_spots, share) * d_low.astype(jnp.float32), axis=1)
    column = lax.psum(column, "cells").reshape(tile_rows, tile_cols)
    d_flat = lax.all_gather(d_low, "cells", axis=1, tiled=True)
    d_map = lax.dot_general(
        cells_expr, d_flat, (((1,), (1,)), ((), ())), preferred_element_type=jnp.float32
    )
    d_map = d_map.reshape(cell_rows, tile_rows, tile_cols)
    d_logits = mapping * (d_map - column)
    d_part = jnp.dot(mapping_low, d_flat, preferred_element_type=jnp.float32)
    d_cells = lax.psum_scatter(d_part, ("sx", "sy"), scatter_dimension=1, tiled=True)
    return (losses, predicted, d_logits, d_cells)


def solution(mesh):
    return jax.shard_map(
        per_device,
        mesh=mesh,
        in_specs=(
            P("cells", "sx", "sy"),
            P("cells", None),
            P("sx", "sy", None),
            P(),
            P("sx", "sy"),
            P(None, "sx", "sy"),
            P(None, "sx", "sy"),
        ),
        out_specs=(P(), P("sx", "sy", "cells"), P("cells", "sx", "sy"), P("cells", ("sx", "sy"))),
        check_vma=False,
    )
```

time: 779 us -> 493 us (0.63); the launches traced: 770 us -> 492 us
  waiting for transfers between devices: 498 us -> 304 us
  matrix products: 97.6 us -> 33.6 us
  other arithmetic: 64 us -> 38.7 us
  blocking collectives: 46.7 us -> 57.7 us
    psum x1 -> x0, waiting for transfers between devices: 294 us -> none  [per_device(): lax.psum(partial_pred, 'cells').reshape(tile_rows, tile_cols, gene_width)]
    reduce_scatter x0 -> x1, waiting for transfers between devices: none -> 139 us  [per_device(): lax.psum_scatter(partial_pred, 'cells', scatter_dimension=1, tiled=True)]
    ppermute x6, waiting for transfers between devices: 120 us -> 25.5 us  [with_halo(): lax.ppermute(head, axis, [((i + 1) % count, i) for i in range(ends)])]
    all_gather x0 -> x1, waiting for transfers between devices: none -> 80.5 us  [per_device(): d_flat = lax.all_gather(d_low, 'cells', axis=1, tiled=True)]
    dot_general x6 -> x0, matrix products: 62.1 us -> none  [the longest x3 46 us: by_slide(): return jnp.einsum('src,sg->rcg', slide_hot, table, precision=HIGH)]
    ppermute x6, waiting for transfers between devices: 46.8 us -> 13.8 us  [with_halo(): lax.ppermute(tail, axis, [(i, (i + 1) % count) for i in range(ends)])]
    psum x2 -> x3, blocking collectives: 29.3 us -> 46.9 us  [the longest x1 23.6 us: per_device(): spot_loss = -lax.psum(jnp.sum(spot_cos), ('sx', 'sy')) / all_spots]
    concatenate x3, other arithmetic: 19.4 us -> 2.21 us  [with_halo(): jnp.concatenate([lax.ppermute(tail, axis, [(i, (i + 1) % count) for i in...]
  transfers between devices with their start and end apart: 14 -> 15, of which waited for: 7 -> 9; matrix products, arithmetic and copies ran while one was open for 6% -> 7% of each run, Pallas kernels for 0% -> 0%
where the time goes in v1:
time: 493 us; the launch traced here: 492 us
  waiting for transfers between devices  304 us (62%)
  blocking collectives  57.7 us (12%)
  other arithmetic  38.7 us (8%)
  matrix products  33.6 us (7%)
  starting transfers between devices  29.3 us (6%)
  between operations  15.5 us (3%)
  local copies, waits for them, and re-layouts  13.4 us (3%)
    reduce_scatter x1, waiting for transfers between devices, per_device(): lax.psum_scatter(partial_pred, 'cells', scatter_dimension=1, tiled=True)  139 us
    all_gather x1, waiting for transfers between devices, per_device(): d_flat = lax.all_gather(d_low, 'cells', axis=1, tiled=True)  80.5 us
    reduce_scatter x1, waiting for transfers between devices, per_device(): lax.psum_scatter(d_part, ('sx', 'sy'), scatter_dimension=1, tiled=True)  44.4 us
    ppermute x6, waiting for transfers between devices, with_halo(): lax.ppermute(head, axis, [((i + 1) % count, i) for i in range(ends)])  25.5 us
    psum x1, blocking collectives, per_device(): spot_loss = -lax.psum(jnp.sum(spot_cos), ('sx', 'sy')) / all_spots  23.6 us
    ppermute x6, starting transfers between devices, with_halo(): lax.ppermute(head, axis, [((i + 1) % count, i) for i in range(ends)])  16.4 us
    psum x1, blocking collectives, per_device(): spot_part = lax.psum(spot_part, 'cells')  14.9 us
    ppermute x6, waiting for transfers between devices, with_halo(): lax.ppermute(tail, axis, [(i, (i + 1) % count) for i in range(ends)])  13.8 us
  transfers between devices with their start and end apart: 15, of which 9 were waited for; matrix products, arithmetic and copies ran while one was open for 7% of the time, Pallas kernels for 0%

profile of v1, /device:TPU:1, one launch (start us, length us, event | category | flops | bytes accessed | tf_op | source)
XLA Modules:
  0.0 491.8 jit_solution(843215727056973190)
XLA Ops:
  7.2 0.0 reduce-scatter.3.cloned.1.call-start
  7.2 4.2 exponential_reduce_fusion
  11.4 10.8 %psum.42 = f32[4,256]{1,0:T(4,128)S(1)} all-reduce(f32[4,256]{1,0:T(4,128)S(1)} %exponential_reduce_fusion), channel_id=1, replica_groups=mesh['sx'=4,'sy'=2,'cells'=4] {'cells'}, use_global_device_ids=true, to_apply=%region_1.0 | all-reduce | flops 1024 | bytes 8192 | tf_op jit(solution)/shard_map/psum | solution.py:44
  22.2 4.1 fusion.38
  26.3 0.0 copy-start.8
  26.3 0.7 copy.13
  27.0 0.0 copy-start.3
  27.0 1.6 copy-done.3
  28.6 1.4 copy-done.8
  30.0 8.9 %fusion.49 = f32[1024,2048]{1,0:T(8,128)} fusion(bf16[1408,1024]{1,0:T(8,128)(2,1)S(1)} %bitcast.120, bf16[1408,2048]{1,0:T(8,128)(2,1)S(1)} %copy-done.8), kind=kOutput, calls=%fused_computation.122 | convolution fusion | flops 5905580032 | bytes 17039360 | tf_op jit(solution)/shard_map/dot_general | solution.py:47
  38.9 0.0 reduce-scatter.3.cloned.1.call-update
  38.9 0.0 all-gather.2.cloned.1.call-start
  39.0 0.7 copy-done.5
  39.6 0.0 copy-done.6
  39.7 3.1 collective-permute-start.4
  42.8 1.3 collective-permute-start.5
  44.1 0.1 fusion.46
  44.2 0.1 convert_reduce_fusion
  44.4 139.3 %reduce-scatter.3.cloned.1.call-done = f32[1024,512]{1,0:T(8,128)} async-done(((f32[1024,2048]{1,0:T(8,128)}), f32[1024,512]{1,0:T(8,128)}) %reduce-scatter.3.cloned.1.call-update) | async-done | bytes 2097168 | tf_op jit(solution)/shard_map/reduce_scatter | solution.py:50
  183.7 1.4 slice_bitcast_fusion.1
  185.1 3.1 collective-permute-start
  188.2 1.3 collective-permute-start.1
  189.6 0.1 fusion.44
  189.7 1.3 collective-permute-start.6
  190.9 3.0 collective-permute-start.10
  194.0 4.6 collective-permute-done
  198.6 13.1 %collective-permute-done.1 = f32[1,256,512]{2,1,0:T(8,128)S(1)} collective-permute-done((f32[1,256,512]{2,1,0:T(8,128)S(1)}, f32[1,256,512]{2,1,0:T(8,128)S(1)}, u32[]{:S(2)}, u32[]{:S(2)}) %collective-permute-start.1) | collective-permute-done | bytes 524320 | tf_op jit(solution)/shard_map/ppermute | solution.py:20
  211.7 3.7 collective-permute-start.2
  215.4 1.3 collective-permute-start.3
  216.7 0.1 maximum_bitcast_fusion.1
  216.9 1.6 collective-permute-done.3
  218.5 1.0 pad_maximum_fusion
  219.5 2.9 fusion.41
  222.3 5.4 %fusion = (f32[4,256]{1,0:T(4,128)S(1)}, f32[4,256]{1,0:T(4,128)S(1)}, f32[4,256]{1,0:T(4,128)S(1)}, f32[4,256,512]{2,1,0:T(8,128)}, f32[4,256,512]{2,1,0:T(8,128)}) fusion(f32[512]{0:T(512)S(1)} %bitcast.132, f32[512]{0:T(512)S(1)} %bitcast.130, pred[4,256]{1,0:T(4,128)(4,1)S(1)} %broadcast_compare_fusion, f32[4,256,512]{2,1,0:T(8,128)S(1)} %get-tuple-element.19, ...), kind=kLoop, calls=%fused_computation.14 | loop fusion | flops 5239808 | bytes 8406020 | tf_op jit(solution)/shard_map/reduce_sum | solution.py:70
  227.7 14.9 %psum.45 = f32[3,4,256]{2,1,0:T(4,128)S(1)} all-reduce(f32[3,4,256]{2,1,0:T(4,128)S(1)} %pad_maximum_fusion.14), channel_id=1, replica_groups=mesh['sx'=4,'sy'=2,'cells'=4] {'cells'}, use_global_device_ids=true, to_apply=%region_14.15 | all-reduce | flops 3072 | bytes 24576 | tf_op jit(solution)/shard_map/psum | solution.py:73
  242.6 0.6 reduce_sum.118
  243.2 3.3 multiply_reduce_fusion.2
  246.6 23.6 %all-reduce = (f32[]{:T(128)}, f32[3,2,512]{2,1,0:T(2,128)S(1)}) all-reduce(f32[]{:T(128)} %reduce_sum.118, f32[3,2,512]{2,1,0:T(2,128)S(1)} %pad_maximum_fusion.13), channel_id=1, replica_groups=mesh['sx'=4,'sy'=2,'cells'=4] {'sx','sy'}, use_global_device_ids=true, to_apply=%region_16.17 | all-reduce | flops 3073 | bytes 24584 | tf_op jit(solution)/shard_map/psum | solution.py:82
  270.2 0.1 multiply_multiply_fusion.1
  270.2 2.7 fusion.3
  273.0 0.1 fusion.43
  273.1 2.5 collective-permute-start.7
  275.6 1.3 collective-permute-start.8
  276.9 7.6 %collective-permute-done.7 = f32[1,256,512]{2,1,0:T(8,128)S(1)} collective-permute-done((f32[1,256,512]{2,1,0:T(8,128)S(1)}, f32[1,256,512]{2,1,0:T(8,128)S(1)}, u32[]{:S(2)}, u32[]{:S(2)}) %collective-permute-start.7) | collective-permute-done | bytes 524320 | tf_op jit(solution)/shard_map/ppermute | solution.py:18
  284.5 11.6 %collective-permute-done.8 = f32[1,256,512]{2,1,0:T(8,128)S(1)} collective-permute-done((f32[1,256,512]{2,1,0:T(8,128)S(1)}, f32[1,256,512]{2,1,0:T(8,128)S(1)}, u32[]{:S(2)}, u32[]{:S(2)}) %collective-permute-start.8) | collective-permute-done | bytes 524320 | tf_op jit(solution)/shard_map/ppermute | solution.py:20
  296.1 1.3 collective-permute-start.9
  297.4 5.8 %collective-permute-start.11 = (f32[6,1,512]{2,1,0:T(1,128)S(1)}, f32[6,1,512]{2,1,0:T(1,128)S(1)}, u32[]{:S(2)}, u32[]{:S(2)}) collective-permute-start(f32[6,1,512]{2,1,0:T(1,128)S(1)} %get-tuple-element.25), channel_id=1, source_target_pairs={{4,0},{5,1},{6,2},{7,3},{12,8},{13,9},{14,10},{15,11},{20,16},{21,... | collective-permute-start | bytes 36872 | tf_op jit(solution)/shard_map/ppermute | solution.py:20
  303.2 0.8 collective-permute-done.11
  304.0 1.2 maximum_maximum_fusion.1
  305.2 2.5 fusion.5
  307.7 0.0 all-gather.2.cloned.1.call-update
  307.8 0.2 reduce-scatter.5.cloned.1.call-start
  308.0 80.5 %all-gather.2.cloned.1.call-done = bf16[1024,2048]{1,0:T(8,128)(2,1)} async-done(((bf16[1024,512]{1,0:T(8,128)(2,1)}), bf16[1024,2048]{1,0:T(8,128)(2,1)}) %all-gather.2.cloned.1.call-update) | async-done | bytes 4194320 | tf_op jit(solution)/shard_map/all_gather | solution.py:115
  388.5 11.3 %fusion.51 = f32[1408,2048]{1,0:T(8,128)} fusion(bf16[1408,1024]{1,0:T(8,128)(2,1)} %bitcast.121, bf16[1024,2048]{1,0:T(8,128)(2,1)} %all-gather.2.cloned.1.call-done), kind=kOutput, calls=%fused_computation.124 | convolution fusion | flops 5905580032 | bytes 18612224 | tf_op jit(solution)/shard_map/dot_general | solution.py:121
  399.8 0.0 reduce-scatter.5.cloned.1.call-update
  400.5 0.1 multiply_reduce_fusion.4
  400.7 0.6 divide_reduce_fusion
  401.9 0.3 multiply_reduce_fusion.3
  402.3 8.5 %all-reduce.1 = (f32[1]{0:T(128)}, f32[4,256]{1,0:T(4,128)S(1)}) all-reduce(f32[1]{0:T(128)} %bitcast.15, f32[4,256]{1,0:T(4,128)S(1)} %sub.10), channel_id=1, replica_groups=mesh['sx'=4,'sy'=2,'cells'=4] {'cells'}, use_global_device_ids=true, to_apply=%region_10.11 | all-reduce | flops 1025 | bytes 8200 | tf_op jit(solution)/shard_map/psum | solution.py:81
  410.8 1.2 pad_maximum_fusion.23
  412.0 13.4 %fusion.50 = f32[1024,1408]{1,0:T(8,128)} fusion(bf16[1024,2048]{1,0:T(8,128)(2,1)} %all-gather.2.cloned.1.call-done, bf16[1408,2048]{1,0:T(8,128)(2,1)} %param.8), kind=kOutput, calls=%fused_computation.123 | convolution fusion | flops 5905580032 | bytes 15728640 | tf_op jit(solution)/shard_map/dot_general | solution.py:116
  425.3 7.4 %copy.12 = f32[1408,4,256]{2,1,0:T(4,128)} copy(f32[1408,4,256]{0,2,1:T(8,128)} %bitcast.119) | data formatting | bytes 11534336 | tf_op jit(solution)/shard_map/reshape | solution.py:119
  432.8 8.1 %subtract_multiply_fusion = f32[704,8,256]{2,1,0:T(8,128)} fusion(f32[704,8,256]{2,1,0:T(8,128)} %bitcast.115, f32[8,256]{1,0:T(8,128)S(1)} %bitcast.127, f32[8,256]{1,0:T(8,128)S(1)} %bitcast.126, f32[704,8,256]{2,1,0:T(8,128)} %bitcast.110), kind=kLoop, calls=%fused_computation | loop fusion | flops 4325376 | bytes 17317888 | tf_op jit(solution)/shard_map/mul | solution.py:120
  440.9 44.4 %reduce-scatter.5.cloned.1.call-done = f32[1408,256]{1,0:T(8,128)} async-done(((f32[1408,2048]{1,0:T(8,128)}), f32[1408,256]{1,0:T(8,128)}) %reduce-scatter.5.cloned.1.call-update) | async-done | bytes 1441808 | tf_op jit(solution)/shard_map/reduce_scatter | solution.py:122
  (35 shorter events, 0.2 us)
Async XLA Ops:
  7.2 176.5 %reduce-scatter.3.cloned.1.call-start = ((), (), s32[]{:S(2)}) async-start(), calls=%async_computation.2 | async-start | bytes 10485760 | tf_op jit(solution)/shard_map/reduce_scatter | solution.py:50
  26.3 3.7 copy-start.8
  27.0 1.6 copy-start.3
  38.9 0.7 copy-start.5
  38.9 0.8 copy-start.6
  38.9 5.2 %copy-start.4 = (s32[2,2048]{1,0:T(2,128)S(1)}, s32[2,2048]{1,0:T(2,128)}, u32[]{:S(2)}) copy-start(s32[2,2048]{1,0:T(2,128)} %param.10) | copy-start | bytes 49156
  38.9 5.4 %copy-start.7 = (s32[4,256]{1,0:T(4,128)S(1)}, s32[4,256]{1,0:T(4,128)}, u32[]{:S(2)}) copy-start(s32[4,256]{1,0:T(4,128)} %param.11) | copy-start | bytes 12292
  38.9 349.5 %all-gather.2.cloned.1.call-start = ((), (), s32[]{:S(2)}) async-start(), calls=%async_computation.3 | async-start | bytes 5242880 | tf_op jit(solution)/shard_map/all_gather | solution.py:115
  39.7 149.8 %collective-permute-start.4 = (f32[6,1,256]{2,1,0:T(1,128)S(1)}, f32[6,1,256]{2,1,0:T(1,128)S(1)}, u32[]{:S(2)}, u32[]{:S(2)}) collective-permute-start(f32[6,1,256]{2,1,0:T(1,128)S(1)} %get-tuple-element.51), channel_id=1, source_target_pairs={{0,8},{8,16},{16,24},{1,9},{9,17},{17,25},{2,10},{10,18},{18,26},{... | collective-permute-start | bytes 18440 | tf_op jit(solution)/shard_map/ppermute | solution.py:18
  42.8 146.7 %collective-permute-start.5 = (f32[6,1,256]{2,1,0:T(1,128)S(1)}, f32[6,1,256]{2,1,0:T(1,128)S(1)}, u32[]{:S(2)}, u32[]{:S(2)}) collective-permute-start(f32[6,1,256]{2,1,0:T(1,128)S(1)} %get-tuple-element.52), channel_id=1, source_target_pairs={{8,0},{16,8},{24,16},{9,1},{17,9},{25,17},{10,2},{18,10},{26,18},{... | collective-permute-start | bytes 18440 | tf_op jit(solution)/shard_map/ppermute | solution.py:20
  183.7 28.0 %copy-start = (f32[1024,512]{1,0:T(8,128)S(1)}, f32[1024,512]{1,0:T(8,128)}, u32[]{:S(2)}) copy-start(f32[1024,512]{1,0:T(8,128)} %reduce-scatter.3.cloned.1.call-done) | copy-start | bytes 6291460
  185.1 13.5 %collective-permute-start = (f32[1,256,512]{2,1,0:T(8,128)S(1)}, f32[1,256,512]{2,1,0:T(8,128)S(1)}, u32[]{:S(2)}, u32[]{:S(2)}) collective-permute-start(f32[1,256,512]{2,1,0:T(8,128)S(1)} %get-tuple-element.32), channel_id=1, source_target_pairs={{0,8},{8,16},{16,24},{1,9},{9,17},{17,25},{2,10},{10,18},{18,26},{... | collective-permute-start | bytes 1572872 | tf_op jit(solution)/shard_map/ppermute | solution.py:18
  188.2 23.5 %collective-permute-start.1 = (f32[1,256,512]{2,1,0:T(8,128)S(1)}, f32[1,256,512]{2,1,0:T(8,128)S(1)}, u32[]{:S(2)}, u32[]{:S(2)}) collective-permute-start(f32[1,256,512]{2,1,0:T(8,128)S(1)} %get-tuple-element.33), channel_id=1, source_target_pairs={{8,0},{16,8},{24,16},{9,1},{17,9},{25,17},{10,2},{18,10},{26,18},{... | collective-permute-start | bytes 1572872 | tf_op jit(solution)/shard_map/ppermute | solution.py:20
  189.7 27.1 %collective-permute-start.6 = (f32[6,6,1]{2,1,0:T(8,128)S(1)}, f32[6,6,1]{2,1,0:T(8,128)S(1)}, u32[]{:S(2)}, u32[]{:S(2)}) collective-permute-start(f32[6,6,1]{2,1,0:T(8,128)S(1)} %get-tuple-element.38), channel_id=1, source_target_pairs={{0,4},{1,5},{2,6},{3,7},{8,12},{9,13},{10,14},{11,15},{16,20},{17,... | collective-permute-start | bytes 440 | tf_op jit(solution)/shard_map/ppermute | solution.py:18
  190.9 25.8 %collective-permute-start.10 = (f32[6,6,1]{2,1,0:T(8,128)S(1)}, f32[6,6,1]{2,1,0:T(8,128)S(1)}, u32[]{:S(2)}, u32[]{:S(2)}) collective-permute-start(f32[6,6,1]{2,1,0:T(8,128)S(1)} %get-tuple-element.39), channel_id=1, source_target_pairs={{4,0},{5,1},{6,2},{7,3},{12,8},{13,9},{14,10},{15,11},{20,16},{21,... | collective-permute-start | bytes 440 | tf_op jit(solution)/shard_map/ppermute | solution.py:20
  211.7 5.1 %collective-permute-start.2 = (f32[6,1,512]{2,1,0:T(1,128)S(1)}, f32[6,1,512]{2,1,0:T(1,128)S(1)}, u32[]{:S(2)}, u32[]{:S(2)}) collective-permute-start(f32[6,1,512]{2,1,0:T(1,128)S(1)} %get-tuple-element.28), channel_id=1, source_target_pairs={{4,0},{5,1},{6,2},{7,3},{12,8},{13,9},{14,10},{15,11},{20,16},{21,... | collective-permute-start | bytes 36872 | tf_op jit(solution)/shard_map/ppermute | solution.py:20
  215.4 3.1 collective-permute-start.3
  222.3 5.4 %copy-start.1 = (f32[4,256,512]{2,1,0:T(8,128)}, f32[4,256,512]{2,1,0:T(8,128)S(1)}, u32[]{:S(2)}) copy-start(f32[4,256,512]{2,1,0:T(8,128)S(1)} %get-tuple-element.19) | copy-start | bytes 6291460
  273.1 11.4 %collective-permute-start.7 = (f32[1,256,512]{2,1,0:T(8,128)S(1)}, f32[1,256,512]{2,1,0:T(8,128)S(1)}, u32[]{:S(2)}, u32[]{:S(2)}) collective-permute-start(f32[1,256,512]{2,1,0:T(8,128)S(1)} %get-tuple-element.30), channel_id=1, source_target_pairs={{0,8},{8,16},{16,24},{1,9},{9,17},{17,25},{2,10},{10,18},{18,26},{... | collective-permute-start | bytes 1572872 | tf_op jit(solution)/shard_map/ppermute | solution.py:18
  275.6 20.5 %collective-permute-start.8 = (f32[1,256,512]{2,1,0:T(8,128)S(1)}, f32[1,256,512]{2,1,0:T(8,128)S(1)}, u32[]{:S(2)}, u32[]{:S(2)}) collective-permute-start(f32[1,256,512]{2,1,0:T(8,128)S(1)} %get-tuple-element.31), channel_id=1, source_target_pairs={{8,0},{16,8},{24,16},{9,1},{17,9},{25,17},{10,2},{18,10},{26,18},{... | collective-permute-start | bytes 1572872 | tf_op jit(solution)/shard_map/ppermute | solution.py:20
  296.1 7.1 %collective-permute-start.9 = (f32[6,1,512]{2,1,0:T(1,128)S(1)}, f32[6,1,512]{2,1,0:T(1,128)S(1)}, u32[]{:S(2)}, u32[]{:S(2)}) collective-permute-start(f32[6,1,512]{2,1,0:T(1,128)S(1)} %get-tuple-element.24), channel_id=1, source_target_pairs={{0,4},{1,5},{2,6},{3,7},{8,12},{9,13},{10,14},{11,15},{16,20},{17,... | collective-permute-start | bytes 36872 | tf_op jit(solution)/shard_map/ppermute | solution.py:18
  297.4 6.6 %collective-permute-start.11 = (f32[6,1,512]{2,1,0:T(1,128)S(1)}, f32[6,1,512]{2,1,0:T(1,128)S(1)}, u32[]{:S(2)}, u32[]{:S(2)}) collective-permute-start(f32[6,1,512]{2,1,0:T(1,128)S(1)} %get-tuple-element.25), channel_id=1, source_target_pairs={{4,0},{5,1},{6,2},{7,3},{12,8},{13,9},{14,10},{15,11},{20,16},{21,... | collective-permute-start | bytes 36872 | tf_op jit(solution)/shard_map/ppermute | solution.py:20
  307.8 177.5 %reduce-scatter.5.cloned.1.call-start = ((), (), s32[]{:S(2)}) async-start(), calls=%async_computation.4 | async-start | bytes 12976128 | tf_op jit(solution)/shard_map/reduce_scatter | solution.py:122
  399.8 2.2 copy-start.2
Sparse Core Ops, SparseCore 0:
  39.1 144.5 reduce-scatter.2
  307.9 80.5 all-gather.1
  399.9 85.2 reduce-scatter.4

commit v2 on v1

v2 whole, which is shorter than its diff:
```python
import functools

import jax
import jax.numpy as jnp
from jax import lax
from jax.experimental import pallas as pl
from jax.experimental.pallas import tpu as pltpu
from jax.sharding import PartitionSpec as P

EPS = 1e-06
OFFSETS = ((0, 1), (0, -1), (1, 0), (-1, 0), (-1, 1), (1, -1))
LANES = 128
TOP = 32767.0
MESH = pl.DeviceIdType.MESH
F32, BF16, I16, I32 = jnp.float32, jnp.bfloat16, jnp.int16, jnp.int32
rem, div = lax.rem, lax.div


def loop(count, body):
    lax.fori_loop(0, count, lambda i, _: (body(i), 0)[1], 0)


def remote(src, dst, sent, got, to):
    return pltpu.make_async_remote_copy(
        src_ref=src, dst_ref=dst, send_sem=sent, recv_sem=got, device_id=to, device_id_type=MESH
    )


def wait(ref, sem):
    pltpu.make_async_copy(ref, ref, sem).wait()


def spread(row):
    parts = [
        jnp.broadcast_to(row[:, at : at + LANES], (LANES, LANES)).T
        for at in range(0, row.shape[1], LANES)
    ]
    return jnp.concatenate(parts, axis=0)


def fold(x):
    return jnp.sum(x.reshape(x.shape[0] // 8, 8, x.shape[1]), axis=0)


def kernel(names, sizes, *refs):
    n, nsx, nsy, share, all_spots = sizes
    o = dict(zip(names, refs, strict=True))
    lg, cells, spat, gmask, slide, ew, em = (o[k] for k in names[:7])
    losses, gp, dlog, dcell = (o[k] for k in names[7:11])
    xs, mm, mt, dm, srow, ab, sc, tt = (o[k] for k in names[11:19])
    gg, sm, sp, pad, hg, hs, hd, hq = (o[k] for k in names[19:27])
    es, er, cf, cb, hot, con, cor, acc = (o[k] for k in names[27:35])
    gs, gr, spx, gc, spr, dd, fm = (o[k] for k in names[35:42])
    pss, rs1, rs2, rs3, dcv, gpr, gps = (o[k] for k in names[42:49])

    c_rows, t_rows, width = lg.shape
    spots = t_rows * width
    nb = cells.shape[1] // 2 // LANES
    wl = width // LANES
    wb = gpr.shape[0]
    nplane = nsx * nsy
    half = nb // 2
    bpg = nb // 4
    tile = LANES
    tiles = c_rows // tile
    quarter = c_rows // t_rows
    sub = min(64, width)
    mid = slice(8, 8 + width)

    sx, sy, cz = (lax.axis_index(a) for a in ("sx", "sy", "cells"))
    here = sx * nsy + sy
    owner = (cz == 0) | (cz == n - 1)
    od = jnp.where(cz == 0, 0, 1)
    up, down = sx > 0, sx < nsx - 1
    mate = (sx, 1 - sy, cz)

    def gene_block(d, k):
        return jnp.where(d == 0, rem(k + half, nb), nb + k)

    for r in range(t_rows):
        pltpu.make_async_copy(lg.at[:, r, :], dm.at[r], o["lg_m"].at[r]).start()

    def load_cells(b):
        at = pl.ds(pl.multiple_of(b * LANES, LANES), LANES)
        return pltpu.make_async_copy(cells.at[:, at], xs.at[b], o["xs_m"].at[b])

    loop(2 * nb, lambda b: load_cells(b).start())

    def load_truth(k):
        at = pl.ds(pl.multiple_of(gene_block(od, k) * LANES, LANES), LANES)
        return pltpu.make_async_copy(spat.at[:, :, at], sp.at[k], o["sp_m"].at[k])

    @pl.when(owner)
    def _():
        loop(nb, lambda k: load_truth(k).start())

    barrier = pltpu.get_barrier_semaphore()

    def greet_line(j):
        to = (sx, sy, rem(cz + j + 1, n))
        pl.semaphore_signal(barrier, inc=1, device_id=to, device_id_type=MESH)

    def greet_plane(j):
        t = rem(here + j + 1, nplane)
        to = (div(t, nsy), rem(t, nsy), cz)
        pl.semaphore_signal(barrier, inc=1, device_id=to, device_id_type=MESH)

    loop(n - 1, greet_line)
    loop(nplane - 1, greet_plane)

    for r in range(t_rows):
        pltpu.make_async_copy(lg.at[:, r, :], dm.at[r], o["lg_m"].at[r]).wait()

        def exps(i, s, r=r):
            at = pl.ds(i * tile, tile)
            x = jnp.exp(dm[r, at, :])
            dm[r, at, :] = x
            return s + fold(x)

        s = lax.fori_loop(0, c_rows // tile, exps, jnp.zeros((8, width), F32))
        s = jnp.sum(s, axis=0, keepdims=True)
        for h in range(wl):
            srow[cz, pl.ds(r * wl + h, 1), :] = s[:, h * LANES : (h + 1) * LANES]

    pl.semaphore_wait(barrier, n - 1 + nplane - 1)

    def send_sums(j):
        to = (sx, sy, rem(cz + j + 1, n))
        remote(srow.at[cz], srow.at[cz], o["s_s"].at[j], o["s_r"].at[cz], to).start()

    loop(n - 1, send_sums)

    def turn(dst, first):
        def each(i):
            for r in range(t_rows):
                at = pl.ds(pl.multiple_of((i + first) * LANES, LANES), LANES)
                dst[i, r] = dm[r, at, :].T

        return each

    turned = ((gg, 0, min(tiles, nb)), (sm, nb, max(tiles - nb, 0)))
    for dst, first, count in turned:
        loop(count, turn(dst, first))

    def wait_sums(j):
        z = rem(cz + j + 1, n)
        wait(srow.at[z], o["s_r"].at[z])

    loop(n - 1, wait_sums)
    total = srow[0]
    for z in range(1, n):
        total = total + srow[z]
    inv = 1.0 / total
    inv_rows = [
        jnp.concatenate([inv[r * wl + h : r * wl + h + 1] for h in range(wl)], axis=1)
        for r in range(t_rows)
    ]
    for r in range(t_rows):
        tt[0, 0, r] = spread(inv_rows[r])

    for dst, first, count in turned:
        def scale(i, dst=dst, first=first):
            at = pl.ds(pl.multiple_of((i + first) * LANES, LANES), LANES)
            for r in range(t_rows):
                mt[r, :, at] = (dst[i, r] * tt[0, 0, r]).astype(BF16)

        loop(count, scale)

    def keep_mapping():
        for r in range(t_rows):
            def each(i, r=r):
                at = pl.ds(pl.multiple_of(i * LANES, LANES), LANES)
                mm[at, r * width : (r + 1) * width] = (dm[r, at, :] * inv_rows[r]).astype(BF16)
                dm[r, at, :] = jnp.zeros((LANES, width), F32)

            loop(tiles, each)

    loop(2 * nb, lambda b: load_cells(b).wait())

    def coef_routes():
        return (
            (0, down, (sx + 1, sy, cz)),
            (1, up, (sx - 1, sy, cz)),
            (2, sx >= 0, mate),
            (3, down, (sx + 1, 1 - sy, cz)),
            (4, up, (sx - 1, 1 - sy, cz)),
        )

    def predict(d, k, r):
        tt[d, rem(k, 2), r] = jnp.dot(mt[r], xs[gene_block(d, k)], preferred_element_type=F32)

    def put(d, k, r, t):
        top = jnp.maximum(jnp.max(jnp.abs(t), axis=0, keepdims=True), 1e-30)
        ab[d, k, r] = jnp.round(t * (TOP / top)).astype(I32).astype(I16)
        sc[d, k, r] = top * (1.0 / TOP)

    def pass_on(d, k, r):
        to = (sx, sy, cz + 2 * d - 1)
        remote(ab.at[d, k, r], ab.at[d, k, r], o["a_s"].at[d, k, r], o["a_r"].at[d, k, r], to).start()
        remote(sc.at[d, k, r], sc.at[d, k, r], o["c_s"].at[d, k, r], o["c_r"].at[d, k, r], to).start()

    def chunk_of(q):
        return div(q, t_rows), rem(rem(q, t_rows) * (t_rows - 1), t_rows)

    @pl.when(owner)
    def _():
        d = 1 - od

        def first(q):
            k, r = chunk_of(q)
            predict(d, k, r)
            put(d, k, r, tt[d, rem(k, 2), r])
            pass_on(d, k, r)

        loop(nb * t_rows, first)

        for r in range(t_rows):
            rows = [ew[j, r : r + 1, :] * em[j, r : r + 1, :].astype(F32) for j in range(6)]
            con[r] = jnp.concatenate(rows + [jnp.zeros((2, width), F32)], axis=0)
            for j in range(6):
                cf[j, r] = spread(rows[j])
            hot[r] = spread(slide[r : r + 1, :].astype(F32))
        acc[...] = jnp.zeros(acc.shape, F32)

        for slot, ok, to in coef_routes():
            @pl.when(ok)
            def _(slot=slot, to=to):
                remote(con, cor.at[slot], o["co_s"].at[slot], o["co_r"].at[slot], to).start()

        loop(nb, lambda k: load_truth(k).wait())

    def back_coefs():
        for slot, ok in ((0, up), (1, down), (2, sx >= 0), (3, up), (4, down)):
            @pl.when(ok)
            def _(slot=slot):
                wait(cor.at[slot], o["co_r"].at[slot])

        lane = lax.broadcasted_iota(I32, (8, width), 1)
        for j, (dr, dc) in enumerate(OFFSETS):
            for r in range(t_rows):
                at = r - dr
                if at < 0:
                    base, side, ok = cor[0, t_rows - 1], cor[3, t_rows - 1], up
                elif at >= t_rows:
                    base, side, ok = cor[1, 0], cor[4, 0], down
                else:
                    base, side, ok = con[at], cor[2, at], sx >= 0
                base = jnp.where(ok, base, 0.0)
                if dc:
                    by, edge = (1, 0) if dc == 1 else (width - 1, width - 1)
                    side = jnp.where(ok & (sy == (1 if dc == 1 else 0)), side, 0.0)
                    base = jnp.where(lane == edge, pltpu.roll(side, by, 1), pltpu.roll(base, by, 1))
                cb[j, r] = spread(base[j : j + 1]).astype(BF16)

    def send_edges(slot, which, k, rows):
        parts = [
            jnp.where(sy == 1, pad[slot, row, 8:9, :], pad[slot, row, 7 + width : 8 + width, :])
            for row in rows
        ]
        parts.append(jnp.zeros((8 - len(parts), LANES), F32))
        es[which, k] = jnp.concatenate(parts, axis=0)
        remote(es.at[which, k], er.at[which, k], o["e_s"].at[which, k], o["e_r"].at[which, k], mate).start()

    def take_edges(slot, which, k, rows):
        wait(er.at[which, k], o["e_r"].at[which, k])
        for i, row in enumerate(rows):
            edge = er[which, k, i : i + 1, :]
            pad[slot, row, 8 + width : 9 + width, :] = jnp.where(sy == 0, edge, 0.0)
            pad[slot, row, 7:8, :] = jnp.where(sy == 1, edge, 0.0)

    sides = ((0, up, 0), (1, down, t_rows + 1))

    def prepare(k):
        for side, ok, row in sides:
            @pl.when(ok)
            def _(side=side, row=row):
                wait(hg.at[side, k], o["hg_r"].at[side, k])
                wait(hs.at[side, k], o["hs_r"].at[side, k])
                pad[0, row, mid, :] = hg[side, k].astype(I32).astype(F32) * hs[side, k]

            @pl.when(jnp.logical_not(ok))
            def _(row=row):
                pad[0, row, mid, :] = jnp.zeros((width, LANES), F32)

        def rows(r):
            pad[0, r + 1, mid, :] = gg[k, r]

        loop(t_rows, rows)
        send_edges(0, 0, k, range(t_rows + 2))

    def smoothing(k):
        take_edges(0, 0, k, range(t_rows + 2))
        at = pl.ds(pl.multiple_of(gene_block(od, k) * LANES, LANES), LANES)
        mask = gmask[:, at].astype(F32)
        m0, m1 = mask[0:1], mask[1:2]

        def rows(r, sums):
            sums = list(sums)
            for u in range(0, width, sub):
                here_u = slice(u, u + sub)
                a = pad[0, r + 1, 8 + u : 8 + u + sub, :]
                for j, (dr, dc) in enumerate(OFFSETS):
                    a = a + cf[j, r, here_u, :] * pad[0, r + 1 + dr, 8 + dc + u : 8 + dc + u + sub, :]
                sm[k, r, here_u, :] = a
                t = sp[k, r, here_u, :]
                h = hot[r, here_u, :]
                mk = m0 + h * (m1 - m0)
                for i, x in enumerate((a * t, a * a, t * t)):
                    sums[2 * i] = sums[2 * i] + fold(x)
                    sums[2 * i + 1] = sums[2 * i + 1] + fold(x * h)
                    acc[i, r, here_u, :] = acc[i, r, here_u, :] + x * mk
            return tuple(sums)

        sums = lax.fori_loop(0, t_rows, rows, (jnp.zeros((8, LANES), F32),) * 6)
        parts = []
        for i in range(3):
            both = jnp.sum(sums[2 * i], axis=0, keepdims=True)
            one = jnp.sum(sums[2 * i + 1], axis=0, keepdims=True)
            parts += [both - one, one]
        gs[k] = jnp.concatenate(parts + [jnp.zeros((2, LANES), F32)], axis=0)

    def own_block(t, i):
        b = div(t * share, LANES) + i - od * nb
        return jnp.where(od == 0, rem(b + half, nb), b)

    def pred_copies(i, j):
        t = jnp.where(od == 0, j + 1, n - 2 - j)
        k = own_block(t, i)
        to = (sx, sy, t)
        return (
            remote(ab.at[od, k], gpr.at[i], o["gp_s"].at[j, i], o["gp_r"].at[i], to),
            remote(sc.at[od, k], gps.at[i], o["gq_s"].at[j, i], o["gq_r"].at[i], to),
        )

    def send_pred(i):
        def each(j):
            for copy in pred_copies(i, j):
                copy.start()

        loop(n // 2 - 1, each)

    early_pred = wb - 1 if n == 4 else 0

    lead = max(n - 3, 0)

    def sum_step(s):
        def direction(d):
            own, first = cz == d * (n - 1), cz == (1 - d) * (n - 1)
            off = jnp.where(owner, 0, jnp.where(d == 1, 2 * (cz - 1), 2 * (n - 2 - cz)))
            q = s - off

            @pl.when(jnp.logical_not(first) & (q >= 0) & (q < nb * t_rows))
            def _():
                k, r = chunk_of(q)
                wait(ab.at[d, k, r], o["a_r"].at[d, k, r])
                wait(sc.at[d, k, r], o["c_r"].at[d, k, r])
                got = ab[d, k, r].astype(I32).astype(F32) * sc[d, k, r]
                t = tt[d, rem(k, 2), r] + got
                put(d, k, r, t)

                @pl.when(jnp.logical_not(own))
                def _():
                    pass_on(d, k, r)

                @pl.when(own)
                def _():
                    gg[k, r] = t
                    for side, ok, row, to in halo_routes():
                        @pl.when(ok & (r == row))
                        def _(side=side, row=row, to=to):
                            remote(ab.at[d, k, row], hg.at[side, k], o["hg_s"].at[side, k], o["hg_r"].at[side, k], to).start()
                            remote(sc.at[d, k, row], hs.at[side, k], o["hs_s"].at[side, k], o["hs_r"].at[side, k], to).start()

                    i = rem(q, t_rows)

                    @pl.when((k > 0) & (i == 1))
                    def _():
                        prepare(k - 1)

                    @pl.when((k > 0) & (i == t_rows - 1))
                    def _():
                        smoothing(k - 1)

                    if early_pred:
                        @pl.when(q == 3 * nb * t_rows // 4)
                        def _():
                            for i in range(early_pred):
                                send_pred(i)

                @pl.when(k + 1 < nb)
                def _():
                    predict(d, k + 1, r)

        loop(2, direction)

        @pl.when(owner & (s == half * t_rows))
        def _():
            back_coefs()

    def halo_routes():
        return ((1, up, 0, (sx - 1, sy, cz)), (0, down, t_rows - 1, (sx + 1, sy, cz)))

    keep_mapping()

    def first_block(d):
        @pl.when(cz != (1 - d) * (n - 1))
        def _():
            loop(t_rows, lambda r: predict(d, 0, r))

    loop(2, first_block)
    loop(nb * t_rows + 2 * lead, sum_step)

    def diff_inside(k):
        slot = rem(k, 2)
        tc0, tc1, sc0, sc1, m0, m1 = (gc[k, i : i + 1, :] for i in range(6))

        def rows(r):
            for u in range(0, width, sub):
                here_u = slice(u, u + sub)
                h = hot[r, here_u, :]
                mk = m0 + h * (m1 - m0)
                by_truth = tc0 + h * (tc1 - tc0) + mk * acc[1, r, here_u, :]
                by_smooth = sc0 + h * (sc1 - sc0) + mk * acc[2, r, here_u, :]
                pad[slot, r + 1, 8 + u : 8 + u + sub, :] = (
                    by_truth * sp[k, r, here_u, :] + by_smooth * sm[k, r, here_u, :]
                )

        loop(t_rows, rows)
        for side, ok, row, to in halo_routes():
            @pl.when(ok)
            def _(side=side, row=row, to=to):
                hq[side, k] = pad[slot, row + 1, mid, :].astype(BF16)
                remote(hq.at[side, k], hd.at[side, k], o["hd_s"].at[side, k], o["hd_r"].at[side, k], to).start()

        send_edges(slot, 1, k, range(1, t_rows + 1))

    def diff_border(k):
        slot = rem(k, 2)
        for side, ok, row in sides:
            @pl.when(ok)
            def _(side=side, row=row):
                wait(hd.at[side, k], o["hd_r"].at[side, k])
                pad[slot, row, mid, :] = hd[side, k].astype(F32)

            @pl.when(jnp.logical_not(ok))
            def _(row=row):
                pad[slot, row, mid, :] = jnp.zeros((width, LANES), F32)

        send_edges(slot, 2, k, (0, t_rows + 1))

    back = cz + 1 - 2 * od

    def diff_pred(k, rows):
        slot = rem(k, 2)
        for r in rows:
            for u in range(0, width, sub):
                here_u = slice(u, u + sub)
                a = pad[slot, r + 1, 8 + u : 8 + u + sub, :]
                for j, (dr, dc) in enumerate(OFFSETS):
                    w = cb[j, r, here_u, :].astype(F32)
                    a = a + w * pad[slot, r + 1 - dr, 8 - dc + u : 8 - dc + u + sub, :]
                low = a.astype(BF16)
                dd[od, k, r, here_u, :] = low
                acc[0, r, here_u, :] = acc[0, r, here_u, :] + gg[k, r, here_u, :] * low.astype(F32)
            at = dd.at[od, k, r]
            remote(at, at, o["d_s"].at[od, k, r], o["d_r"].at[od, k, r], (sx, sy, back)).start()

    def back_chunk(q):
        i = rem(q, t_rows)
        return div(q, t_rows), jnp.where(i < t_rows - 2, i + 1, jnp.where(i == t_rows - 2, 0, i))

    def spot_rows(i):
        return [
            jnp.sum(acc[i, r, h * LANES : (h + 1) * LANES, :].T, axis=0, keepdims=True)
            for r in range(t_rows)
            for h in range(wl)
        ]

    def plane_peer(j):
        t = rem(here + j + 1, nplane)
        return t, (div(t, nsy), rem(t, nsy), cz)

    def put_own(i):
        k = own_block(cz, i)
        return pltpu.make_async_copy(gg.at[k], gp.at[:, :, i * LANES : (i + 1) * LANES], o["gp_m"].at[i])

    @pl.when(owner)
    def _():
        prepare(nb - 1)
        smoothing(nb - 1)

        def send_genes(j):
            _, to = plane_peer(j)
            remote(gs, gr.at[here], o["g_s"].at[j], o["g_r"].at[here], to).start()

        loop(nplane - 1, send_genes)
        for i in range(3):
            for at, row in enumerate(spot_rows(i)):
                spx[0, i, at : at + 1, :] = row
        remote(spx.at[0], spx.at[1], o["x_s"].at[0], o["x_r"].at[0], (sx, sy, n - 1 - cz)).start()
        if early_pred:
            for i in range(early_pred, wb):
                send_pred(i)
        gr[here] = gs[...]
        for i in range(wb):
            put_own(i).start()

        def wait_genes(j):
            t, _ = plane_peer(j)
            wait(gr.at[t], o["g_r"].at[t])

        loop(nplane - 1, wait_genes)
        count = jnp.maximum(jnp.sum(gmask[...].astype(F32), axis=1, keepdims=True), 1.0)

        def genes(k, gl):
            tot = gr[0, k]
            for t in range(1, nplane):
                tot = tot + gr[t, k]
            ib, ic = lax.rsqrt(tot[2:4] + EPS), lax.rsqrt(tot[4:6] + EPS)
            cos = tot[0:2] * ib * ic
            at = pl.ds(pl.multiple_of(gene_block(od, k) * LANES, LANES), LANES)
            mask = gmask[:, at].astype(F32)
            scale = -mask / (2.0 * count)
            gc[k, 0:2, :] = scale * ib * ic
            gc[k, 2:4, :] = -scale * cos * ib * ib
            gc[k, 4:6, :] = mask
            return gl + mask * cos / count

        gl = lax.fori_loop(0, nb, genes, jnp.zeros((2, LANES), F32))
        gene_part = jnp.sum(jnp.sum(gl, axis=0, keepdims=True), axis=1, keepdims=True)

        wait(spx.at[1], o["x_r"].at[0])
        a, b, c = (spx[0, i] + spx[1, i] for i in range(3))
        ib, ic = lax.rsqrt(b + EPS), lax.rsqrt(c + EPS)
        cos = a * ib * ic
        by_truth = (-1.0 / all_spots) * ib * ic
        by_smooth = (1.0 / all_spots) * cos * ib * ib
        for r in range(t_rows):
            for h in range(wl):
                at, i = slice(h * LANES, (h + 1) * LANES), r * wl + h
                acc[1, r, at, :] = spread(by_truth[i : i + 1])
                acc[2, r, at, :] = spread(by_smooth[i : i + 1])
        acc[0] = jnp.zeros(acc.shape[1:], F32)
        spot_part = jnp.sum(jnp.sum(cos, axis=0, keepdims=True), axis=1, keepdims=True)
        spr[here] = jnp.broadcast_to(spot_part, (8, LANES))

        def send_spot(j):
            _, to = plane_peer(j)
            remote(spr.at[here], spr.at[here], o["p_s"].at[j], o["p_r"].at[here], to).start()

        diff_inside(0)
        loop(nplane - 1, send_spot)

        def produce(k):
            take_edges(rem(k, 2), 1, k, range(1, t_rows + 1))
            diff_pred(k, range(1, t_rows - 1))

            @pl.when(k + 1 < nb)
            def _():
                diff_inside(k + 1)

            diff_border(k)
            take_edges(rem(k, 2), 2, k, (0, t_rows + 1))
            diff_pred(k, (0, t_rows - 1))

        loop(nb, produce)

        def wait_spot(j):
            t, _ = plane_peer(j)
            wait(spr.at[t], o["p_r"].at[t])

        loop(nplane - 1, wait_spot)
        spot_all = spr[0, 0:1, :]
        for t in range(1, nplane):
            spot_all = spot_all + spr[t, 0:1, :]
        rows = spot_rows(0)
        if len(rows) < 8:
            rows.append(jnp.zeros((8 - len(rows), LANES), F32))
        fm[od, 0] = jnp.concatenate(rows, axis=0)
        last = [jnp.broadcast_to(gene_part, (1, LANES)), spot_all, jnp.zeros((6, LANES), F32)]
        fm[od, 1] = jnp.concatenate(last, axis=0)
        remote(fm.at[od], fm.at[od], o["f_s"].at[od], o["f_r"].at[od], (sx, sy, back)).start()
        if not early_pred:
            for i in range(wb):
                send_pred(i)


    sy_bit, sx_bit = div(sx, 2), rem(sx, 2)
    over_y, over_x = (sx + 2 - 4 * sy_bit, sy, cz), (sx + 1 - 2 * sx_bit, sy, cz)

    def place(k):
        jj = div(k, bpg)
        hi = div(jj, 2)
        return rem(jj, 2) == sy, hi * bpg + rem(k, bpg), jnp.where(sy_bit == 0, 1 - hi, hi) == sx_bit

    halves = (pl.ds(0, c_rows // 2), pl.ds(c_rows // 2, c_rows // 2))

    def add_rows(dst, a, b):
        count = dst.shape[0] // 2

        def rows(i):
            at = pl.ds(pl.multiple_of(i * count, 8), count)
            dst[at, :] = (a[at, :].astype(F32) + b[at, :].astype(F32)).astype(dst.dtype)

        loop(2, rows)

    def scatter_0(k):
        mine, at, _ = place(k)

        @pl.when(jnp.logical_not(mine))
        def _():
            for d in range(2):
                remote(pss.at[rem(k, 2), d], rs1.at[d, at], o["r1_s"].at[d, at], o["r1_r"].at[d, at], mate).start()

    def stays(final):
        return sy_bit, jnp.where(final, sy_bit, 1 - sy_bit)

    def scatter_1(k):
        mine, at, final = place(k)

        @pl.when(mine)
        def _():
            def each(d):
                wait(rs1.at[d, at], o["r1_r"].at[d, at])
                add_rows(rs1.at[d, at], pss.at[rem(k, 2), d], rs1.at[d, at])

            loop(2, each)
            for h, (d, to) in enumerate(zip(stays(final), (over_y, over_x), strict=True)):
                src, dst = rs1.at[1 - d, at, halves[h]], rs2.at[at, halves[h]]
                remote(src, dst, o["r2_s"].at[h, at], o["r2_r"].at[h, at], to).start()

        @pl.when(jnp.logical_not(mine))
        def _():
            for d in range(2):
                wait(pss.at[rem(k, 2), d], o["r1_s"].at[d, at])

    def scatter_2(k):
        mine, at, final = place(k)

        @pl.when(mine)
        def _():
            i = rem(k, bpg)
            for h, (d, to) in enumerate(zip(stays(final), (over_x, over_y), strict=True)):
                part = rs2.at[at, halves[h]]
                wait(part, o["r2_r"].at[h, at])
                add_rows(part, rs1.at[d, at, halves[h]], part)

                @pl.when(jnp.logical_not(final))
                def _(h=h, part=part, to=to):
                    remote(part, rs3.at[i, halves[h]], o["r3_s"].at[h, i], o["r3_r"].at[h, i], to).start()

            for h, d in enumerate(stays(final)):
                wait(rs1.at[1 - d, at, halves[h]], o["r2_s"].at[h, at])

    def put_cells(i):
        at = pl.ds(pl.multiple_of(i * LANES, LANES), LANES)
        return pltpu.make_async_copy(dcv.at[i], dcell.at[:, at], o["dc_m"].at[i])

    def scatter_3(k):
        mine, at, final = place(k)
        i = rem(k, bpg)

        @pl.when(mine & final)
        def _():
            for h in range(2):
                wait(rs3.at[i, halves[h]], o["r3_r"].at[h, i])
                add_rows(dcv.at[i, halves[h]], rs2.at[at, halves[h]], rs3.at[i, halves[h]])
            put_cells(i).start()

        @pl.when(mine & jnp.logical_not(final))
        def _():
            for h in range(2):
                wait(rs2.at[at, halves[h]], o["r3_s"].at[h, i])

    def multiply(k, piece):
        x = jnp.concatenate([xs[gene_block(0, k)], xs[gene_block(1, k)]], axis=1)
        d = jnp.concatenate([dd[0, k, piece], dd[1, k, piece]], axis=1)
        dm[piece] += lax.dot_general(x, d, (((1,), (1,)), ((), ())), preferred_element_type=F32)
        at = pl.ds(pl.multiple_of(piece * quarter, 16 if quarter % 16 == 0 else 8), quarter)
        d = jnp.concatenate([dd[i, k].reshape(spots, LANES) for i in range(2)], axis=1)
        out = jnp.dot(mm[at, :], d, preferred_element_type=F32).astype(BF16)
        pss[rem(k, 2), 0, at, :] = out[:, :LANES]
        pss[rem(k, 2), 1, at, :] = out[:, LANES:]

    def put_logits(r):
        return pltpu.make_async_copy(dm.at[r], dlog.at[:, r, :], o["dl_m"].at[r])

    def finish(r):
        col = jnp.concatenate([fm[0, 0, i : i + 1] + fm[1, 0, i : i + 1] for i in range(r * wl, (r + 1) * wl)], axis=1)

        def rows(i):
            at = pl.ds(pl.multiple_of(i * tile, tile), tile)
            low = mm[at, r * width : (r + 1) * width].astype(F32)
            dm[r, at, :] = low * (dm[r, at, :] - col)

        loop(c_rows // tile, rows)
        put_logits(r).start()

    def put_pred(i):
        return pltpu.make_async_copy(gg.at[i], gp.at[:, :, i * LANES : (i + 1) * LANES], o["gp_m"].at[i])

    def take_pred(i):
        wait(gpr.at[i], o["gp_r"].at[i])
        wait(gps.at[i], o["gq_r"].at[i])

        def rows(r):
            gg[i, r] = gpr[i, r].astype(I32).astype(F32) * gps[i, r]

        loop(t_rows, rows)
        put_pred(i).start()

    lag = jnp.where(owner, 0, 2 * jnp.maximum(cz - 1, n - 2 - cz))

    def back_step(s):
        def direction(d):
            own, end = cz == d * (n - 1), cz == (1 - d) * (n - 1)
            off = jnp.where(owner, 0, jnp.where(d == 0, 2 * (cz - 1), 2 * (n - 2 - cz)))
            q = s - off
            to = (sx, sy, cz + 1 - 2 * d)

            @pl.when(jnp.logical_not(own) & (q >= 0) & (q < nb * t_rows))
            def _():
                k, r = back_chunk(q)
                at = dd.at[d, k, r]
                wait(at, o["d_r"].at[d, k, r])

                @pl.when(jnp.logical_not(end))
                def _():
                    remote(at, at, o["d_s"].at[d, k, r], o["d_r"].at[d, k, r], to).start()

            @pl.when(jnp.logical_not(own) & (q == nb * t_rows))
            def _():
                wait(fm.at[d], o["f_r"].at[d])

                @pl.when(jnp.logical_not(end))
                def _():
                    remote(fm.at[d], fm.at[d], o["f_s"].at[d], o["f_r"].at[d], to).start()

        loop(2, direction)
        w = s - lag - t_rows
        k, piece = div(w, t_rows), rem(w, t_rows)

        @pl.when((w >= 0) & (k < nb))
        def _():
            multiply(k, piece)

            @pl.when(piece == t_rows - 1)
            def _():
                scatter_0(k)

        @pl.when((w >= 0) & (k == nb))
        def _():
            for r in range(t_rows):
                @pl.when(piece == r)
                def _(r=r):
                    finish(r)

        for stage, back_by, at in ((scatter_1, 1, 0), (scatter_2, 2, 1), (scatter_3, 3, 2)):
            @pl.when((w >= 0) & (piece == at) & (k >= back_by) & (k < nb + back_by))
            def _(stage=stage, back_by=back_by):
                stage(k - back_by)

    loop(t_rows * (nb + 4) + 2 * lead, back_step)

    losses[0] = jnp.max(fm[0, 1, 0:1, :] + fm[1, 1, 0:1, :]) * -0.5
    losses[1] = jnp.max(fm[0, 1, 1:2, :]) * (-1.0 / all_spots)

    @pl.when(jnp.logical_not(owner))
    def _():
        for i in range(wb):
            take_pred(i)

    for r in range(t_rows):
        put_logits(r).wait()
    for i in range(bpg):
        put_cells(i).wait()
    loop(n - 1, lambda j: wait(srow.at[cz], o["s_s"].at[j]))

    def sent(d):
        own, end = cz == d * (n - 1), cz == (1 - d) * (n - 1)

        @pl.when(jnp.logical_not(own))
        def _():
            def each(q):
                k, r = div(q, t_rows), rem(q, t_rows)
                wait(ab.at[d, k, r], o["a_s"].at[d, k, r])
                wait(sc.at[d, k, r], o["c_s"].at[d, k, r])

            loop(nb * t_rows, each)

        @pl.when(jnp.logical_not(end))
        def _():
            def each(q):
                k, r = div(q, t_rows), rem(q, t_rows)
                wait(dd.at[d, k, r], o["d_s"].at[d, k, r])

            loop(nb * t_rows, each)
            wait(fm.at[d], o["f_s"].at[d])

    loop(2, sent)

    @pl.when(jnp.logical_not(owner))
    def _():
        for i in range(wb):
            put_pred(i).wait()

    @pl.when(owner)
    def _():
        for i in range(wb):
            put_own(i).wait()

            def each(j, i=i):
                for copy in pred_copies(i, j):
                    copy.wait_send()

            loop(n // 2 - 1, each)
        for slot, ok, _ in coef_routes():
            @pl.when(ok)
            def _(slot=slot):
                wait(con, o["co_s"].at[slot])

        def each(k):
            for side, ok, row, _ in halo_routes():
                @pl.when(ok)
                def _(side=side, row=row):
                    wait(ab.at[od, k, row], o["hg_s"].at[side, k])
                    wait(sc.at[od, k, row], o["hs_s"].at[side, k])
                    wait(hq.at[side, k], o["hd_s"].at[side, k])

            for which in range(3):
                wait(es.at[which, k], o["e_s"].at[which, k])

        loop(nb, each)
        wait(spx.at[0], o["x_s"].at[0])

        def each_peer(j):
            wait(gs, o["g_s"].at[j])
            wait(spr.at[here], o["p_s"].at[j])

        loop(nplane - 1, each_peer)


def per_device(logits, cells_expr, spatial, gene_mask, slide_id, edge_weight, edge_mask):
    c_rows, t_rows, width = logits.shape
    genes = cells_expr.shape[1]
    n, nsx, nsy = (lax.axis_size(a) for a in ("cells", "sx", "sy"))
    spots = t_rows * width
    share = genes // n
    wide = max(share, LANES)
    wb = wide // LANES
    nb = genes // 2 // LANES
    nplane = nsx * nsy
    grid = (t_rows, width, LANES)
    vm, dma = pltpu.VMEM, pltpu.SemaphoreType.DMA
    scratch = dict(
        xs=vm((2 * nb, c_rows, LANES), BF16),
        mm=vm((c_rows, spots), BF16),
        mt=vm((t_rows, width, c_rows), BF16),
        dm=vm((t_rows, c_rows, width), F32),
        srow=vm((n, spots // LANES, LANES), F32),
        ab=vm((2, nb, *grid), I16),
        sc=vm((2, nb, t_rows, 1, LANES), F32),
        tt=vm((2, 2, *grid), F32),
        gg=vm((nb, *grid), F32),
        sm=vm((nb, *grid), F32),
        sp=vm((nb, *grid), F32),
        pad=vm((2, t_rows + 2, width + 16, LANES), F32),
        hg=vm((2, nb, width, LANES), I16),
        hs=vm((2, nb, 1, LANES), F32),
        hd=vm((2, nb, width, LANES), BF16),
        hq=vm((2, nb, width, LANES), BF16),
        es=vm((3, nb, 8, LANES), F32),
        er=vm((3, nb, 8, LANES), F32),
        cf=vm((6, *grid), F32),
        cb=vm((6, *grid), BF16),
        hot=vm(grid, F32),
        con=vm((t_rows, 8, width), F32),
        cor=vm((5, t_rows, 8, width), F32),
        acc=vm((3, *grid), F32),
        gs=vm((nb, 8, LANES), F32),
        gr=vm((nplane, nb, 8, LANES), F32),
        spx=vm((2, 3, spots // LANES, LANES), F32),
        gc=vm((nb, 8, LANES), F32),
        spr=vm((nplane, 8, LANES), F32),
        dd=vm((2, nb, *grid), BF16),
        fm=vm((2, 2, 8, LANES), F32),
        pss=vm((2, 2, c_rows, LANES), BF16),
        rs1=vm((2, nb // 2, c_rows, LANES), BF16),
        rs2=vm((nb // 2, c_rows, LANES), BF16),
        rs3=vm((nb // 4, c_rows, LANES), BF16),
        dcv=vm((nb // 4, c_rows, LANES), F32),
        gpr=vm((wb, *grid), I16),
        gps=vm((wb, t_rows, 1, LANES), F32),
        lg_m=dma((t_rows,)),
        xs_m=dma((2 * nb,)),
        sp_m=dma((nb,)),
        s_s=dma((n,)),
        s_r=dma((n,)),
        a_s=dma((2, nb, t_rows)),
        a_r=dma((2, nb, t_rows)),
        c_s=dma((2, nb, t_rows)),
        c_r=dma((2, nb, t_rows)),
        hg_s=dma((2, nb)),
        hg_r=dma((2, nb)),
        hs_s=dma((2, nb)),
        hs_r=dma((2, nb)),
        hd_s=dma((2, nb)),
        hd_r=dma((2, nb)),
        e_s=dma((3, nb)),
        e_r=dma((3, nb)),
        co_s=dma((5,)),
        co_r=dma((5,)),
        g_s=dma((nplane,)),
        g_r=dma((nplane,)),
        p_s=dma((nplane,)),
        p_r=dma((nplane,)),
        x_s=dma((1,)),
        x_r=dma((1,)),
        d_s=dma((2, nb, t_rows)),
        d_r=dma((2, nb, t_rows)),
        f_s=dma((2,)),
        f_r=dma((2,)),
        r1_s=dma((2, nb // 2)),
        r1_r=dma((2, nb // 2)),
        r2_s=dma((2, nb // 2)),
        r2_r=dma((2, nb // 2)),
        r3_s=dma((2, nb // 4)),
        r3_r=dma((2, nb // 4)),
        gp_s=dma((max(n // 2 - 1, 1), wb)),
        gp_r=dma((wb,)),
        gq_s=dma((max(n // 2 - 1, 1), wb)),
        gq_r=dma((wb,)),
        gp_m=dma((wb,)),
        dl_m=dma((t_rows,)),
        dc_m=dma((nb // 4,)),
    )
    names = ("lg", "cells", "spat", "gmask", "slide", "ew", "em", "losses", "gp", "dlog", "dcell")
    names += tuple(scratch)
    sizes = (n, nsx, nsy, share, spots * nplane)
    anywhere, local = pl.BlockSpec(memory_space=pl.ANY), pl.BlockSpec(memory_space=pltpu.VMEM)
    losses, pred, d_logits, d_cells = pl.pallas_call(
        functools.partial(kernel, names, sizes),
        out_shape=(
            jax.ShapeDtypeStruct((2,), F32),
            jax.ShapeDtypeStruct((t_rows, width, wide), F32),
            jax.ShapeDtypeStruct(logits.shape, F32),
            jax.ShapeDtypeStruct((c_rows, genes // nplane), F32),
        ),
        in_specs=[anywhere] * 3 + [local] * 4,
        out_specs=(pl.BlockSpec(memory_space=pltpu.SMEM), anywhere, anywhere, anywhere),
        scratch_shapes=list(scratch.values()),
        compiler_params=pltpu.CompilerParams(
            collective_id=0, has_side_effects=True, vmem_limit_bytes=VMEM
        ),
        cost_estimate=pl.CostEstimate(
            flops=6 * c_rows * spots * genes, bytes_accessed=32 << 20, transcendentals=c_rows * spots
        ),
    )(logits, cells_expr, spatial, gene_mask, slide_id, edge_weight, edge_mask)
    if wide > share:
        pred = lax.dynamic_slice_in_dim(pred, rem(lax.axis_index("cells") * share, wide), share, 2)
    return (losses, pred, d_logits, d_cells)


VMEM = 64 * 1024 * 1024 - 512 * 1024


def solution(mesh):
    return jax.shard_map(
        per_device,
        mesh=mesh,
        in_specs=(
            P("cells", "sx", "sy"),
            P("cells", None),
            P("sx", "sy", None),
            P(),
            P("sx", "sy"),
            P(None, "sx", "sy"),
            P(None, "sx", "sy"),
        ),
        out_specs=(P(), P("sx", "sy", "cells"), P("cells", "sx", "sy"), P("cells", ("sx", "sy"))),
        check_vma=False,
    )
```

time: 493 us -> 180 us (0.37)
  waiting for transfers between devices: 304 us -> 0 us
  Pallas kernels: 0 us -> 168 us
  blocking collectives: 57.7 us -> 0 us
  other arithmetic: 38.7 us -> 0 us
  matrix products: 33.6 us -> 0 us
  starting transfers between devices: 29.3 us -> 0 us
  between operations: 15.5 us -> 0.64 us
    reduce_scatter x2 -> x0, waiting for transfers between devices: 184 us -> none  [the longest x1 139 us: per_device(): lax.psum_scatter(partial_pred, 'cells', scatter_dimension=1, tiled=True)]
    pallas_call x0 -> x1, Pallas kernels: none -> 168 us  [per_device(): pl.pallas_call(functools.partial(kernel, names, sizes), out_shape=(jax.Sh...]
    all_gather x1 -> x0, waiting for transfers between devices: 80.5 us -> none  [per_device(): d_flat = lax.all_gather(d_low, 'cells', axis=1, tiled=True)]
    psum x4 -> x0, blocking collectives: 57.7 us -> none  [the longest x1 23.6 us: per_device(): spot_loss = -lax.psum(jnp.sum(spot_cos), ('sx', 'sy')) / all_spots]
    ppermute x12 -> x0, waiting for transfers between devices: 39.4 us -> none  [the longest x6 25.5 us: with_halo(): lax.ppermute(head, axis, [((i + 1) % count, i) for i in range(ends)])]
    dot_general x3 -> x0, matrix products: 33.6 us -> none  [the longest x1 13.4 us: per_device(): lax.dot_general(cells_expr, d_flat, (((1,), (1,)), ((), ())), preferred_e...]
    ppermute x12 -> x0, starting transfers between devices: 29 us -> none  [the longest x6 16.4 us: with_halo(): lax.ppermute(head, axis, [((i + 1) % count, i) for i in range(ends)])]
    reduce_sum x8 -> x0, other arithmetic: 14.7 us -> none  [the longest x1 5.38 us: per_device(): jnp.sum(spot_mask * what, axis=-1)]
  transfers between devices with their start and end apart: 15 -> 0, of which waited for: 9 -> 0; matrix products, arithmetic and copies ran while one was open for 7% -> 0% of each run, Pallas kernels for 0% -> 0%
where the time goes in v2:
time: 180 us
  Pallas kernels  168 us (93%)
  local copies, waits for them, and re-layouts  11.9 us (7%)
    pallas_call x1, Pallas kernels, per_device(): pl.pallas_call(functools.partial(kernel, names, sizes), out_shape=(jax.Sh...  168 us
    unnamed x6, local copies, waits for them, and re-layouts  11.9 us

profile of v2, /device:TPU:1, one launch (start us, length us, event | category | flops | bytes accessed | tf_op | source)
XLA Modules:
  0.0 180.1 jit_solution(9168348851964087253)
XLA Ops:
  0.6 167.6 %shard_map.102 = (f32[2]{0:T(128)}, f32[4,256,512]{2,1,0:T(8,128)}, f32[1408,4,256]{2,1,0:T(4,128)}, f32[1408,256]{1,0:T(8,128)}) custom-call(f32[1408,4,256]{2,1,0:T(4,128)} %refs_0_.1, bf16[1408,2048]{1,0:T(8,128)(2,1)} %refs_1_.1, f32[4,256,2048]{2,1,0:T(8,128)} %refs_2_.1, s32[2,2048]{1,0:T(2,128)} %refs_3_.1, s32[4,256]{1,0:T(4,128)} %refs_4_.1, ...), custom_call_target="tpu_custom_call" | custom-call | flops 17716740096 | bytes 33554432 | tf_op jit(solution)/shard_map/pallas_call | solution.py:941
  168.3 1.1 copy.15
  169.4 3.1 %copy.16 = f32[4,256,512]{2,1,0:T(8,128)} copy(f32[4,256,512]{2,1,0:T(8,128)} %get-tuple-element.9) | data formatting | bytes 4194304
  172.5 0.0 copy-start
  172.5 6.5 %copy.17 = f32[1408,4,256]{2,1,0:T(4,128)} copy(f32[1408,4,256]{2,1,0:T(4,128)} %get-tuple-element.10) | data formatting | bytes 11534336
  179.0 0.0 copy-done
  179.0 1.1 copy.18
Async XLA Ops:
  172.5 6.6 %copy-start = (f32[1408,256]{1,0:T(8,128)S(1)}, f32[1408,256]{1,0:T(8,128)}, u32[]{:S(2)}) copy-start(f32[1408,256]{1,0:T(8,128)} %get-tuple-element.11) | copy-start | bytes 4325380

commit v3 on v2

--- a/solution.py
+++ b/solution.py
@@ -156,13 +156,13 @@
         for r in range(t_rows)
     ]
     for r in range(t_rows):
-        tt[0, 0, r] = spread(inv_rows[r])
+        acc[0, r] = spread(inv_rows[r])
 
     for dst, first, count in turned:
         def scale(i, dst=dst, first=first):
             at = pl.ds(pl.multiple_of((i + first) * LANES, LANES), LANES)
             for r in range(t_rows):
-                mt[r, :, at] = (dst[i, r] * tt[0, 0, r]).astype(BF16)
+                mt[r, :, at] = (dst[i, r] * acc[0, r]).astype(BF16)
 
         loop(count, scale)
 
@@ -171,11 +171,11 @@
             def each(i, r=r):
                 at = pl.ds(pl.multiple_of(i * LANES, LANES), LANES)
                 mm[at, r * width : (r + 1) * width] = (dm[r, at, :] * inv_rows[r]).astype(BF16)
-                dm[r, at, :] = jnp.zeros((LANES, width), F32)
 
             loop(tiles, each)
 
     loop(2 * nb, lambda b: load_cells(b).wait())
+    keep_mapping()
 
     def coef_routes():
         return (
@@ -186,8 +186,17 @@
             (4, up, (sx - 1, 1 - sy, cz)),
         )
 
-    def predict(d, k, r):
-        tt[d, rem(k, 2), r] = jnp.dot(mt[r], xs[gene_block(d, k)], preferred_element_type=F32)
+    ahead = dm if tt.shape[0] == 1 else tt
+
+    def predict(d, pair, r):
+        g = gene_block(d, 2 * pair)
+        w = jnp.concatenate([xs[g], xs[g + 1]], axis=1)
+        at = pl.ds(pl.multiple_of((2 * d + rem(pair, 2)) * width, 8), width)
+        ahead[r, at, :] = jnp.dot(mt[r], w, preferred_element_type=F32)
+
+    def predicted(d, k, r):
+        at = pl.ds(pl.multiple_of((2 * d + rem(div(k, 2), 2)) * width, 8), width)
+        return ahead[r, at, pl.ds(pl.multiple_of(rem(k, 2) * LANES, LANES), LANES)]
 
     def put(d, k, r, t):
         top = jnp.maximum(jnp.max(jnp.abs(t), axis=0, keepdims=True), 1e-30)
@@ -208,8 +217,12 @@
 
         def first(q):
             k, r = chunk_of(q)
-            predict(d, k, r)
-            put(d, k, r, tt[d, rem(k, 2), r])
+
+            @pl.when(rem(k, 2) == 0)
+            def _():
+                predict(d, div(k, 2), r)
+
+            put(d, k, r, predicted(d, k, r))
             pass_on(d, k, r)
 
         loop(nb * t_rows, first)
@@ -339,14 +352,30 @@
 
         loop(n // 2 - 1, each)
 
-    early_pred = wb - 1 if n == 4 else 0
+    early_pred = 1 if n == 4 else 0
+
+    def plane_peer(j):
+        t = rem(here + j + 1, nplane)
+        return t, (div(t, nsy), rem(t, nsy), cz)
+
+    gene_parts = (pl.ds(0, nb - 1), pl.ds(nb - 1, 1))
+
+    def send_genes(part):
+        at = gene_parts[part]
+
+        def each(j):
+            _, to = plane_peer(j)
+            sems = o["g_s"].at[part, j], o["g_r"].at[part, here]
+            remote(gs.at[at], gr.at[here, at], *sems, to).start()
+
+        loop(nplane - 1, each)
 
     lead = max(n - 3, 0)
 
     def sum_step(s):
         def direction(d):
             own, first = cz == d * (n - 1), cz == (1 - d) * (n - 1)
-            off = jnp.where(owner, 0, jnp.where(d == 1, 2 * (cz - 1), 2 * (n - 2 - cz)))
+            off = jnp.where(owner, 0, LAG_SUM * jnp.where(d == 1, cz - 1, n - 2 - cz))
             q = s - off
 
             @pl.when(jnp.logical_not(first) & (q >= 0) & (q < nb * t_rows))
@@ -355,7 +384,7 @@
                 wait(ab.at[d, k, r], o["a_r"].at[d, k, r])
                 wait(sc.at[d, k, r], o["c_r"].at[d, k, r])
                 got = ab[d, k, r].astype(I32).astype(F32) * sc[d, k, r]
-                t = tt[d, rem(k, 2), r] + got
+                t = predicted(d, k, r) + got
                 put(d, k, r, t)
 
                 @pl.when(jnp.logical_not(own))
@@ -381,15 +410,19 @@
                     def _():
                         smoothing(k - 1)
 
+                    @pl.when((k == nb - 1) & (i == t_rows - 1))
+                    def _():
+                        send_genes(0)
+
                     if early_pred:
                         @pl.when(q == 3 * nb * t_rows // 4)
                         def _():
                             for i in range(early_pred):
                                 send_pred(i)
 
-                @pl.when(k + 1 < nb)
+                @pl.when((rem(k, 2) == d) & (k + 2 - rem(k, 2) < nb))
                 def _():
-                    predict(d, k + 1, r)
+                    predict(d, div(k, 2) + 1, r)
 
         loop(2, direction)
 
@@ -400,38 +433,38 @@
     def halo_routes():
         return ((1, up, 0, (sx - 1, sy, cz)), (0, down, t_rows - 1, (sx + 1, sy, cz)))
 
-    keep_mapping()
-
     def first_block(d):
         @pl.when(cz != (1 - d) * (n - 1))
         def _():
             loop(t_rows, lambda r: predict(d, 0, r))
 
     loop(2, first_block)
-    loop(nb * t_rows + 2 * lead, sum_step)
-
-    def diff_inside(k):
-        slot = rem(k, 2)
+    loop(nb * t_rows + LAG_SUM * lead, sum_step)
+
+    def diff_smooth(k, r, at):
         tc0, tc1, sc0, sc1, m0, m1 = (gc[k, i : i + 1, :] for i in range(6))
-
-        def rows(r):
-            for u in range(0, width, sub):
-                here_u = slice(u, u + sub)
-                h = hot[r, here_u, :]
-                mk = m0 + h * (m1 - m0)
-                by_truth = tc0 + h * (tc1 - tc0) + mk * acc[1, r, here_u, :]
-                by_smooth = sc0 + h * (sc1 - sc0) + mk * acc[2, r, here_u, :]
-                pad[slot, r + 1, 8 + u : 8 + u + sub, :] = (
-                    by_truth * sp[k, r, here_u, :] + by_smooth * sm[k, r, here_u, :]
-                )
-
-        loop(t_rows, rows)
+        h = hot[r, at, :]
+        mk = m0 + h * (m1 - m0)
+        by_truth = tc0 + h * (tc1 - tc0) + mk * acc[1, r, at, :]
+        by_smooth = sc0 + h * (sc1 - sc0) + mk * acc[2, r, at, :]
+        return by_truth * sp[k, r, at, :] + by_smooth * sm[k, r, at, :]
+
+    def send_borders(k):
         for side, ok, row, to in halo_routes():
             @pl.when(ok)
             def _(side=side, row=row, to=to):
-                hq[side, k] = pad[slot, row + 1, mid, :].astype(BF16)
+                for u in range(0, width, sub):
+                    hq[side, k, u : u + sub, :] = diff_smooth(k, row, slice(u, u + sub)).astype(BF16)
                 remote(hq.at[side, k], hd.at[side, k], o["hd_s"].at[side, k], o["hd_r"].at[side, k], to).start()
 
+    def diff_inside(k):
+        slot = rem(k, 2)
+
+        def rows(r):
+            for u in range(0, width, sub):
+                pad[slot, r + 1, 8 + u : 8 + u + sub, :] = diff_smooth(k, r, slice(u, u + sub))
+
+        loop(t_rows, rows)
         send_edges(slot, 1, k, range(1, t_rows + 1))
 
     def diff_border(k):
@@ -469,6 +502,15 @@
         i = rem(q, t_rows)
         return div(q, t_rows), jnp.where(i < t_rows - 2, i + 1, jnp.where(i == t_rows - 2, 0, i))
 
+    def diff_inner(k):
+        take_edges(rem(k, 2), 1, k, range(1, t_rows + 1))
+        diff_pred(k, range(1, t_rows - 1))
+        diff_border(k)
+
+    def diff_outer(k):
+        take_edges(rem(k, 2), 2, k, (0, t_rows + 1))
+        diff_pred(k, (0, t_rows - 1))
+
     def spot_rows(i):
         return [
             jnp.sum(acc[i, r, h * LANES : (h + 1) * LANES, :].T, axis=0, keepdims=True)
@@ -476,10 +518,6 @@
             for h in range(wl)
         ]
 
-    def plane_peer(j):
-        t = rem(here + j + 1, nplane)
-        return t, (div(t, nsy), rem(t, nsy), cz)
-
     def put_own(i):
         k = own_block(cz, i)
         return pltpu.make_async_copy(gg.at[k], gp.at[:, :, i * LANES : (i + 1) * LANES], o["gp_m"].at[i])
@@ -489,25 +527,19 @@
         prepare(nb - 1)
         smoothing(nb - 1)
 
-        def send_genes(j):
-            _, to = plane_peer(j)
-            remote(gs, gr.at[here], o["g_s"].at[j], o["g_r"].at[here], to).start()
-
-        loop(nplane - 1, send_genes)
+        send_genes(1)
         for i in range(3):
             for at, row in enumerate(spot_rows(i)):
                 spx[0, i, at : at + 1, :] = row
         remote(spx.at[0], spx.at[1], o["x_s"].at[0], o["x_r"].at[0], (sx, sy, n - 1 - cz)).start()
-        if early_pred:
-            for i in range(early_pred, wb):
-                send_pred(i)
         gr[here] = gs[...]
         for i in range(wb):
             put_own(i).start()
 
         def wait_genes(j):
             t, _ = plane_peer(j)
-            wait(gr.at[t], o["g_r"].at[t])
+            for part, at in enumerate(gene_parts):
+                wait(gr.at[t, at], o["g_r"].at[part, t])
 
         loop(nplane - 1, wait_genes)
         count = jnp.maximum(jnp.sum(gmask[...].astype(F32), axis=1, keepdims=True), 1.0)
@@ -543,28 +575,22 @@
         acc[0] = jnp.zeros(acc.shape[1:], F32)
         spot_part = jnp.sum(jnp.sum(cos, axis=0, keepdims=True), axis=1, keepdims=True)
         spr[here] = jnp.broadcast_to(spot_part, (8, LANES))
+        fm[od, 1] = jnp.broadcast_to(gene_part, (8, LANES))
 
         def send_spot(j):
             _, to = plane_peer(j)
             remote(spr.at[here], spr.at[here], o["p_s"].at[j], o["p_r"].at[here], to).start()
 
+        send_borders(0)
         diff_inside(0)
+        send_borders(1)
+        take_edges(0, 1, 0, range(1, t_rows + 1))
+        diff_pred(0, range(1, t_rows - 1))
+        loop(nb - 2, lambda k: send_borders(k + 2))
         loop(nplane - 1, send_spot)
-
-        def produce(k):
-            take_edges(rem(k, 2), 1, k, range(1, t_rows + 1))
-            diff_pred(k, range(1, t_rows - 1))
-
-            @pl.when(k + 1 < nb)
-            def _():
-                diff_inside(k + 1)
-
-            diff_border(k)
-            take_edges(rem(k, 2), 2, k, (0, t_rows + 1))
-            diff_pred(k, (0, t_rows - 1))
-
-        loop(nb, produce)
-
+        diff_border(0)
+
+    def send_last():
         def wait_spot(j):
             t, _ = plane_peer(j)
             wait(spr.at[t], o["p_r"].at[t])
@@ -577,12 +603,10 @@
         if len(rows) < 8:
             rows.append(jnp.zeros((8 - len(rows), LANES), F32))
         fm[od, 0] = jnp.concatenate(rows, axis=0)
-        last = [jnp.broadcast_to(gene_part, (1, LANES)), spot_all, jnp.zeros((6, LANES), F32)]
-        fm[od, 1] = jnp.concatenate(last, axis=0)
+        fm[od, 1, 1:2, :] = spot_all
         remote(fm.at[od], fm.at[od], o["f_s"].at[od], o["f_r"].at[od], (sx, sy, back)).start()
-        if not early_pred:
-            for i in range(wb):
-                send_pred(i)
+        for i in range(early_pred, wb):
+            send_pred(i)
 
 
     sy_bit, sx_bit = div(sx, 2), rem(sx, 2)
@@ -672,15 +696,17 @@
             for h in range(2):
                 wait(rs2.at[at, halves[h]], o["r3_s"].at[h, i])
 
+    def add_map(k, r):
+        x = jnp.concatenate([xs[gene_block(0, k)], xs[gene_block(1, k)]], axis=1)
+        d = jnp.concatenate([dd[0, k, r], dd[1, k, r]], axis=1)
+        new = lax.dot_general(x, d, (((1,), (1,)), ((), ())), preferred_element_type=F32)
+        dm[r] = jnp.where(k == 0, 0.0, dm[r]) + new
+
     def multiply(k, piece):
-        x = jnp.concatenate([xs[gene_block(0, k)], xs[gene_block(1, k)]], axis=1)
-        d = jnp.concatenate([dd[0, k, piece], dd[1, k, piece]], axis=1)
-        dm[piece] += lax.dot_general(x, d, (((1,), (1,)), ((), ())), preferred_element_type=F32)
-        at = pl.ds(pl.multiple_of(piece * quarter, 16 if quarter % 16 == 0 else 8), quarter)
         d = jnp.concatenate([dd[i, k].reshape(spots, LANES) for i in range(2)], axis=1)
-        out = jnp.dot(mm[at, :], d, preferred_element_type=F32).astype(BF16)
-        pss[rem(k, 2), 0, at, :] = out[:, :LANES]
-        pss[rem(k, 2), 1, at, :] = out[:, LANES:]
+        out = jnp.dot(mm[...], d, preferred_element_type=F32).astype(BF16)
+        pss[rem(k, 2), 0] = out[:, :LANES]
+        pss[rem(k, 2), 1] = out[:, LANES:]
 
     def put_logits(r):
         return pltpu.make_async_copy(dm.at[r], dlog.at[:, r, :], o["dl_m"].at[r])
@@ -709,12 +735,34 @@
         loop(t_rows, rows)
         put_pred(i).start()
 
-    lag = jnp.where(owner, 0, 2 * jnp.maximum(cz - 1, n - 2 - cz))
+    behind = BEHIND * t_rows
+    lag = jnp.where(owner, behind, LAG_BACK * jnp.maximum(cz - 1, n - 2 - cz))
+
+    def produce(k, piece):
+        @pl.when(piece == 0)
+        def _():
+            diff_outer(k)
+
+        @pl.when((piece == 1) & (k + 1 < nb))
+        def _():
+            diff_inside(k + 1)
+
+        @pl.when((piece == 2) & (k + 1 < nb))
+        def _():
+            diff_inner(k + 1)
+
+        @pl.when((piece == 1) & (k + 1 == nb))
+        def _():
+            send_last()
 
     def back_step(s):
+        @pl.when(owner & (s < nb * t_rows))
+        def _():
+            produce(div(s, t_rows), rem(s, t_rows))
+
         def direction(d):
             own, end = cz == d * (n - 1), cz == (1 - d) * (n - 1)
-            off = jnp.where(owner, 0, jnp.where(d == 0, 2 * (cz - 1), 2 * (n - 2 - cz)))
+            off = jnp.where(owner, behind, LAG_BACK * jnp.where(d == 0, cz - 1, n - 2 - cz))
             q = s - off
             to = (sx, sy, cz + 1 - 2 * d)
 
@@ -737,15 +785,20 @@
                     remote(fm.at[d], fm.at[d], o["f_s"].at[d], o["f_r"].at[d], to).start()
 
         loop(2, direction)
-        w = s - lag - t_rows
+        q = s - lag
+
+        @pl.when((q >= 0) & (q < nb * t_rows))
+        def _():
+            add_map(*back_chunk(q))
+
+        w = q - t_rows
         k, piece = div(w, t_rows), rem(w, t_rows)
 
         @pl.when((w >= 0) & (k < nb))
         def _():
-            multiply(k, piece)
-
-            @pl.when(piece == t_rows - 1)
+            @pl.when(piece == 0)
             def _():
+                multiply(k, piece)
                 scatter_0(k)
 
         @pl.when((w >= 0) & (k == nb))
@@ -755,12 +808,12 @@
                 def _(r=r):
                     finish(r)
 
-        for stage, back_by, at in ((scatter_1, 1, 0), (scatter_2, 2, 1), (scatter_3, 3, 2)):
+        for stage, back_by, at in ((scatter_1, 0, 2), (scatter_2, 1, 2), (scatter_3, 2, 2)):
             @pl.when((w >= 0) & (piece == at) & (k >= back_by) & (k < nb + back_by))
             def _(stage=stage, back_by=back_by):
                 stage(k - back_by)
 
-    loop(t_rows * (nb + 4) + 2 * lead, back_step)
+    loop(t_rows * (nb + 4) + max(LAG_BACK * lead, behind), back_step)
 
     losses[0] = jnp.max(fm[0, 1, 0:1, :] + fm[1, 1, 0:1, :]) * -0.5
     losses[1] = jnp.max(fm[0, 1, 1:2, :]) * (-1.0 / all_spots)
@@ -834,7 +887,8 @@
         wait(spx.at[0], o["x_s"].at[0])
 
         def each_peer(j):
-            wait(gs, o["g_s"].at[j])
+            for part, at in enumerate(gene_parts):
+                wait(gs.at[at], o["g_s"].at[part, j])
             wait(spr.at[here], o["p_s"].at[j])
 
         loop(nplane - 1, each_peer)
@@ -852,6 +906,7 @@
     nplane = nsx * nsy
     grid = (t_rows, width, LANES)
     vm, dma = pltpu.VMEM, pltpu.SemaphoreType.DMA
+    fits = width == 2 * LANES and c_rows >= 4 * width
     scratch = dict(
         xs=vm((2 * nb, c_rows, LANES), BF16),
         mm=vm((c_rows, spots), BF16),
@@ -860,7 +915,7 @@
         srow=vm((n, spots // LANES, LANES), F32),
         ab=vm((2, nb, *grid), I16),
         sc=vm((2, nb, t_rows, 1, LANES), F32),
-        tt=vm((2, 2, *grid), F32),
+        tt=vm((1, 8, LANES) if fits else (t_rows, 4 * width, 2 * LANES), F32),
         gg=vm((nb, *grid), F32),
         sm=vm((nb, *grid), F32),
         sp=vm((nb, *grid), F32),
@@ -910,8 +965,8 @@
         e_r=dma((3, nb)),
         co_s=dma((5,)),
         co_r=dma((5,)),
-        g_s=dma((nplane,)),
-        g_r=dma((nplane,)),
+        g_s=dma((2, nplane)),
+        g_r=dma((2, nplane)),
         p_s=dma((nplane,)),
         p_r=dma((nplane,)),
         x_s=dma((1,)),
@@ -961,6 +1016,9 @@
     return (losses, pred, d_logits, d_cells)
 
 
+BEHIND = 3
+LAG_SUM = 3
+LAG_BACK = 3
 VMEM = 64 * 1024 * 1024 - 512 * 1024
 
 

time: 180 us -> 165 us (0.917)
  Pallas kernels: 168 us -> 152 us
    pallas_call x1, Pallas kernels: 168 us -> 152 us  [per_device(): pl.pallas_call(functools.partial(kernel, names, sizes), out_shape=(jax.Sh...]
where the time goes in v3:
time: 165 us
  Pallas kernels  152 us (92%)
  local copies, waits for them, and re-layouts  11.9 us (7%)
    pallas_call x1, Pallas kernels, per_device(): pl.pallas_call(functools.partial(kernel, names, sizes), out_shape=(jax.Sh...  152 us
    unnamed x6, local copies, waits for them, and re-layouts  11.9 us

profile of v3, /device:TPU:1, one launch (start us, length us, event | category | flops | bytes accessed | tf_op | source)
XLA Modules:
  0.0 164.8 jit_solution(12804237222862314502)
XLA Ops:
  0.6 152.3 %shard_map.102 = (f32[2]{0:T(128)}, f32[4,256,512]{2,1,0:T(8,128)}, f32[1408,4,256]{2,1,0:T(4,128)}, f32[1408,256]{1,0:T(8,128)}) custom-call(f32[1408,4,256]{2,1,0:T(4,128)} %refs_0_.1, bf16[1408,2048]{1,0:T(8,128)(2,1)} %refs_1_.1, f32[4,256,2048]{2,1,0:T(8,128)} %refs_2_.1, s32[2,2048]{1,0:T(2,128)} %refs_3_.1, s32[4,256]{1,0:T(4,128)} %refs_4_.1, ...), custom_call_target="tpu_custom_call" | custom-call | flops 17716740096 | bytes 33554432 | tf_op jit(solution)/shard_map/pallas_call | solution.py:996
  152.9 1.1 copy.15
  154.0 3.1 %copy.16 = f32[4,256,512]{2,1,0:T(8,128)} copy(f32[4,256,512]{2,1,0:T(8,128)} %get-tuple-element.9) | data formatting | bytes 4194304
  157.1 0.0 copy-start
  157.1 6.5 %copy.17 = f32[1408,4,256]{2,1,0:T(4,128)} copy(f32[1408,4,256]{2,1,0:T(4,128)} %get-tuple-element.10) | data formatting | bytes 11534336
  163.7 0.0 copy-done
  163.7 1.1 copy.18
Async XLA Ops:
  157.1 6.6 %copy-start = (f32[1408,256]{1,0:T(8,128)S(1)}, f32[1408,256]{1,0:T(8,128)}, u32[]{:S(2)}) copy-start(f32[1408,256]{1,0:T(8,128)} %get-tuple-element.11) | copy-start | bytes 4325380

commit v4 on v3

--- a/solution.py
+++ b/solution.py
@@ -51,7 +51,7 @@
     gg, sm, sp, pad, hg, hs, hd, hq = (o[k] for k in names[19:27])
     es, er, cf, cb, hot, con, cor, acc = (o[k] for k in names[27:35])
     gs, gr, spx, gc, spr, dd, fm = (o[k] for k in names[35:42])
-    pss, rs1, rs2, rs3, dcv, gpr, gps = (o[k] for k in names[42:49])
+    pss, rs1, rs2, rs3, dcv, gpr, gps, gpb = (o[k] for k in names[42:50])
 
     c_rows, t_rows, width = lg.shape
     spots = t_rows * width
@@ -175,7 +175,6 @@
             loop(tiles, each)
 
     loop(2 * nb, lambda b: load_cells(b).wait())
-    keep_mapping()
 
     def coef_routes():
         return (
@@ -186,17 +185,16 @@
             (4, up, (sx - 1, 1 - sy, cz)),
         )
 
-    ahead = dm if tt.shape[0] == 1 else tt
 
     def predict(d, pair, r):
         g = gene_block(d, 2 * pair)
         w = jnp.concatenate([xs[g], xs[g + 1]], axis=1)
         at = pl.ds(pl.multiple_of((2 * d + rem(pair, 2)) * width, 8), width)
-        ahead[r, at, :] = jnp.dot(mt[r], w, preferred_element_type=F32)
+        tt[r, at, :] = jnp.dot(mt[r], w, preferred_element_type=F32)
 
     def predicted(d, k, r):
         at = pl.ds(pl.multiple_of((2 * d + rem(div(k, 2), 2)) * width, 8), width)
-        return ahead[r, at, pl.ds(pl.multiple_of(rem(k, 2) * LANES, LANES), LANES)]
+        return tt[r, at, pl.ds(pl.multiple_of(rem(k, 2) * LANES, LANES), LANES)]
 
     def put(d, k, r, t):
         top = jnp.maximum(jnp.max(jnp.abs(t), axis=0, keepdims=True), 1e-30)
@@ -439,6 +437,7 @@
             loop(t_rows, lambda r: predict(d, 0, r))
 
     loop(2, first_block)
+    keep_mapping()
     loop(nb * t_rows + LAG_SUM * lead, sum_step)
 
     def diff_smooth(k, r, at):
@@ -518,9 +517,18 @@
             for h in range(wl)
         ]
 
+    def put_pred(i):
+        at = slice(i * LANES, (i + 1) * LANES)
+        return pltpu.make_async_copy(gpb.at[i], gp.at[:, :, at], o["gp_m"].at[i])
+
     def put_own(i):
         k = own_block(cz, i)
-        return pltpu.make_async_copy(gg.at[k], gp.at[:, :, i * LANES : (i + 1) * LANES], o["gp_m"].at[i])
+
+        def rows(r):
+            gpb[i, r] = gg[k, r].astype(BF16)
+
+        loop(t_rows, rows)
+        put_pred(i).start()
 
     @pl.when(owner)
     def _():
@@ -533,9 +541,6 @@
                 spx[0, i, at : at + 1, :] = row
         remote(spx.at[0], spx.at[1], o["x_s"].at[0], o["x_r"].at[0], (sx, sy, n - 1 - cz)).start()
         gr[here] = gs[...]
-        for i in range(wb):
-            put_own(i).start()
-
         def wait_genes(j):
             t, _ = plane_peer(j)
             for part, at in enumerate(gene_parts):
@@ -709,28 +714,26 @@
         pss[rem(k, 2), 1] = out[:, LANES:]
 
     def put_logits(r):
-        return pltpu.make_async_copy(dm.at[r], dlog.at[:, r, :], o["dl_m"].at[r])
+        return pltpu.make_async_copy(mm.at[:, r * width : (r + 1) * width], dlog.at[r], o["dl_m"].at[r])
 
     def finish(r):
         col = jnp.concatenate([fm[0, 0, i : i + 1] + fm[1, 0, i : i + 1] for i in range(r * wl, (r + 1) * wl)], axis=1)
 
         def rows(i):
             at = pl.ds(pl.multiple_of(i * tile, tile), tile)
-            low = mm[at, r * width : (r + 1) * width].astype(F32)
-            dm[r, at, :] = low * (dm[r, at, :] - col)
+            cols = slice(r * width, (r + 1) * width)
+            low = mm[at, cols].astype(F32)
+            mm[at, cols] = (low * (dm[r, at, :] - col)).astype(BF16)
 
         loop(c_rows // tile, rows)
         put_logits(r).start()
-
-    def put_pred(i):
-        return pltpu.make_async_copy(gg.at[i], gp.at[:, :, i * LANES : (i + 1) * LANES], o["gp_m"].at[i])
 
     def take_pred(i):
         wait(gpr.at[i], o["gp_r"].at[i])
         wait(gps.at[i], o["gq_r"].at[i])
 
         def rows(r):
-            gg[i, r] = gpr[i, r].astype(I32).astype(F32) * gps[i, r]
+            gpb[i, r] = (gpr[i, r].astype(I32).astype(F32) * gps[i, r]).astype(BF16)
 
         loop(t_rows, rows)
         put_pred(i).start()
@@ -755,7 +758,72 @@
         def _():
             send_last()
 
+    def drain():
+        loop(n - 1, lambda j: wait(srow.at[cz], o["s_s"].at[j]))
+
+        def sent(d):
+            own, end = cz == d * (n - 1), cz == (1 - d) * (n - 1)
+
+            @pl.when(jnp.logical_not(own))
+            def _():
+                def each(q):
+                    k, r = div(q, t_rows), rem(q, t_rows)
+                    wait(ab.at[d, k, r], o["a_s"].at[d, k, r])
+                    wait(sc.at[d, k, r], o["c_s"].at[d, k, r])
+
+                loop(nb * t_rows, each)
+
+            @pl.when(jnp.logical_not(end))
+            def _():
+                def each(q):
+                    k, r = div(q, t_rows), rem(q, t_rows)
+                    wait(dd.at[d, k, r], o["d_s"].at[d, k, r])
+
+                loop(nb * t_rows, each)
+                wait(fm.at[d], o["f_s"].at[d])
+
+        loop(2, sent)
+
+        @pl.when(owner)
+        def _():
+            for i in range(wb):
+                def each(j, i=i):
+                    for copy in pred_copies(i, j):
+                        copy.wait_send()
+
+                loop(n // 2 - 1, each)
+            for slot, ok, _ in coef_routes():
+                @pl.when(ok)
+                def _(slot=slot):
+                    wait(con, o["co_s"].at[slot])
+
+            def each(k):
+                for side, ok, row, _ in halo_routes():
+                    @pl.when(ok)
+                    def _(side=side, row=row):
+                        wait(ab.at[od, k, row], o["hg_s"].at[side, k])
+                        wait(sc.at[od, k, row], o["hs_s"].at[side, k])
+                        wait(hq.at[side, k], o["hd_s"].at[side, k])
+
+                for which in range(3):
+                    wait(es.at[which, k], o["e_s"].at[which, k])
+
+            loop(nb, each)
+            wait(spx.at[0], o["x_s"].at[0])
+
+            def each_peer(j):
+                for part, at in enumerate(gene_parts):
+                    wait(gs.at[at], o["g_s"].at[part, j])
+                wait(spr.at[here], o["p_s"].at[j])
+
+            loop(nplane - 1, each_peer)
+
     def back_step(s):
+        for i in range(wb):
+            @pl.when(owner & (s == 2 * i + 1))
+            def _(i=i):
+                put_own(i)
+
         @pl.when(owner & (s < nb * t_rows))
         def _():
             produce(div(s, t_rows), rem(s, t_rows))
@@ -776,7 +844,7 @@
                 def _():
                     remote(at, at, o["d_s"].at[d, k, r], o["d_r"].at[d, k, r], to).start()
 
-            @pl.when(jnp.logical_not(own) & (q == nb * t_rows))
+            @pl.when(jnp.logical_not(own) & (q == nb * t_rows + 2))
             def _():
                 wait(fm.at[d], o["f_r"].at[d])
 
@@ -813,85 +881,32 @@
             def _(stage=stage, back_by=back_by):
                 stage(k - back_by)
 
+        @pl.when(w == nb * t_rows + t_rows - 1)
+        def _():
+            drain()
+
+        @pl.when((w == (nb + 1) * t_rows) & jnp.logical_not(owner))
+        def _():
+            for i in range(wb):
+                take_pred(i)
+
     loop(t_rows * (nb + 4) + max(LAG_BACK * lead, behind), back_step)
 
     losses[0] = jnp.max(fm[0, 1, 0:1, :] + fm[1, 1, 0:1, :]) * -0.5
     losses[1] = jnp.max(fm[0, 1, 1:2, :]) * (-1.0 / all_spots)
-
-    @pl.when(jnp.logical_not(owner))
-    def _():
-        for i in range(wb):
-            take_pred(i)
 
     for r in range(t_rows):
         put_logits(r).wait()
     for i in range(bpg):
         put_cells(i).wait()
-    loop(n - 1, lambda j: wait(srow.at[cz], o["s_s"].at[j]))
-
-    def sent(d):
-        own, end = cz == d * (n - 1), cz == (1 - d) * (n - 1)
-
-        @pl.when(jnp.logical_not(own))
-        def _():
-            def each(q):
-                k, r = div(q, t_rows), rem(q, t_rows)
-                wait(ab.at[d, k, r], o["a_s"].at[d, k, r])
-                wait(sc.at[d, k, r], o["c_s"].at[d, k, r])
-
-            loop(nb * t_rows, each)
-
-        @pl.when(jnp.logical_not(end))
-        def _():
-            def each(q):
-                k, r = div(q, t_rows), rem(q, t_rows)
-                wait(dd.at[d, k, r], o["d_s"].at[d, k, r])
-
-            loop(nb * t_rows, each)
-            wait(fm.at[d], o["f_s"].at[d])
-
-    loop(2, sent)
-
-    @pl.when(jnp.logical_not(owner))
-    def _():
-        for i in range(wb):
-            put_pred(i).wait()
-
-    @pl.when(owner)
-    def _():
-        for i in range(wb):
-            put_own(i).wait()
-
-            def each(j, i=i):
-                for copy in pred_copies(i, j):
-                    copy.wait_send()
-
-            loop(n // 2 - 1, each)
-        for slot, ok, _ in coef_routes():
-            @pl.when(ok)
-            def _(slot=slot):
-                wait(con, o["co_s"].at[slot])
-
-        def each(k):
-            for side, ok, row, _ in halo_routes():
-                @pl.when(ok)
-                def _(side=side, row=row):
-                    wait(ab.at[od, k, row], o["hg_s"].at[side, k])
-                    wait(sc.at[od, k, row], o["hs_s"].at[side, k])
-                    wait(hq.at[side, k], o["hd_s"].at[side, k])
-
-            for which in range(3):
-                wait(es.at[which, k], o["e_s"].at[which, k])
-
-        loop(nb, each)
-        wait(spx.at[0], o["x_s"].at[0])
-
-        def each_peer(j):
-            for part, at in enumerate(gene_parts):
-                wait(gs.at[at], o["g_s"].at[part, j])
-            wait(spr.at[here], o["p_s"].at[j])
-
-        loop(nplane - 1, each_peer)
+
+    for i in range(wb):
+        put_pred(i).wait()
+
+
+def cells_first(x, out):
+    for r in range(x.shape[0]):
+        out[:, r, :] = x[r].astype(F32)
 
 
 def per_device(logits, cells_expr, spatial, gene_mask, slide_id, edge_weight, edge_mask):
@@ -906,7 +921,6 @@
     nplane = nsx * nsy
     grid = (t_rows, width, LANES)
     vm, dma = pltpu.VMEM, pltpu.SemaphoreType.DMA
-    fits = width == 2 * LANES and c_rows >= 4 * width
     scratch = dict(
         xs=vm((2 * nb, c_rows, LANES), BF16),
         mm=vm((c_rows, spots), BF16),
@@ -915,7 +929,7 @@
         srow=vm((n, spots // LANES, LANES), F32),
         ab=vm((2, nb, *grid), I16),
         sc=vm((2, nb, t_rows, 1, LANES), F32),
-        tt=vm((1, 8, LANES) if fits else (t_rows, 4 * width, 2 * LANES), F32),
+        tt=vm((t_rows, 4 * width, 2 * LANES), F32),
         gg=vm((nb, *grid), F32),
         sm=vm((nb, *grid), F32),
         sp=vm((nb, *grid), F32),
@@ -943,9 +957,10 @@
         rs1=vm((2, nb // 2, c_rows, LANES), BF16),
         rs2=vm((nb // 2, c_rows, LANES), BF16),
         rs3=vm((nb // 4, c_rows, LANES), BF16),
-        dcv=vm((nb // 4, c_rows, LANES), F32),
+        dcv=vm((nb // 4, c_rows, LANES), BF16),
         gpr=vm((wb, *grid), I16),
         gps=vm((wb, t_rows, 1, LANES), F32),
+        gpb=vm((wb, *grid), BF16),
         lg_m=dma((t_rows,)),
         xs_m=dma((2 * nb,)),
         sp_m=dma((nb,)),
@@ -997,9 +1012,9 @@
         functools.partial(kernel, names, sizes),
         out_shape=(
             jax.ShapeDtypeStruct((2,), F32),
-            jax.ShapeDtypeStruct((t_rows, width, wide), F32),
-            jax.ShapeDtypeStruct(logits.shape, F32),
-            jax.ShapeDtypeStruct((c_rows, genes // nplane), F32),
+            jax.ShapeDtypeStruct((t_rows, width, wide), BF16),
+            jax.ShapeDtypeStruct((t_rows, c_rows, width), BF16),
+            jax.ShapeDtypeStruct((c_rows, genes // nplane), BF16),
         ),
         in_specs=[anywhere] * 3 + [local] * 4,
         out_specs=(pl.BlockSpec(memory_space=pltpu.SMEM), anywhere, anywhere, anywhere),
@@ -1013,7 +1028,16 @@
     )(logits, cells_expr, spatial, gene_mask, slide_id, edge_weight, edge_mask)
     if wide > share:
         pred = lax.dynamic_slice_in_dim(pred, rem(lax.axis_index("cells") * share, wide), share, 2)
-    return (losses, pred, d_logits, d_cells)
+    tile = c_rows // 2 if c_rows % 64 == 0 else c_rows
+    d_logits = pl.pallas_call(
+        cells_first,
+        grid=(c_rows // tile,),
+        out_shape=jax.ShapeDtypeStruct(logits.shape, F32),
+        in_specs=[pl.BlockSpec((t_rows, tile, width), lambda i: (0, i, 0))],
+        out_specs=pl.BlockSpec((tile, t_rows, width), lambda i: (i, 0, 0)),
+        compiler_params=pltpu.CompilerParams(vmem_limit_bytes=60 * 1024 * 1024),
+    )(d_logits)
+    return (losses, pred.astype(F32), d_logits, d_cells.astype(F32))
 
 
 BEHIND = 3

time: 165 us -> 160 us (0.970)
  local copies, waits for them, and re-layouts: 11.9 us -> 0.52 us
  Pallas kernels: 152 us -> 156 us
  other arithmetic: 0 us -> 2.82 us
    unnamed x6 -> x7, local copies, waits for them, and re-layouts: 11.9 us -> 0.52 us
    pallas_call x0 -> x1, Pallas kernels: none -> 4.86 us  [per_device(): pl.pallas_call(cells_first, grid=(c_rows // tile,), out_shape=jax.ShapeDt...]
    convert_element_type x0 -> x2, other arithmetic: none -> 2.82 us  [per_device(): return (losses, pred.astype(F32), d_logits, d_cells.astype(F32))]
where the time goes in v4:
time: 160 us
  Pallas kernels  156 us (98%)
  other arithmetic  2.82 us (2%)
    pallas_call x1, Pallas kernels, per_device(): pl.pallas_call(functools.partial(kernel, names, sizes), out_shape=(jax.Sh...  151 us
    pallas_call x1, Pallas kernels, per_device(): pl.pallas_call(cells_first, grid=(c_rows // tile,), out_shape=jax.ShapeDt...  4.86 us

profile of v4, /device:TPU:1, one launch (start us, length us, event | category | flops | bytes accessed | tf_op | source)
XLA Modules:
  0.0 160.2 jit_solution(12836944239348085646)
XLA Ops:
  0.6 151.3 %shard_map.102 = (f32[2]{0:T(128)}, bf16[4,256,512]{2,1,0:T(8,128)(2,1)}, bf16[4,1408,256]{2,1,0:T(8,128)(2,1)}, bf16[1408,256]{1,0:T(8,128)(2,1)}) custom-call(f32[1408,4,256]{2,1,0:T(4,128)} %refs_0_.1, bf16[1408,2048]{1,0:T(8,128)(2,1)} %refs_1_.1, f32[4,256,2048]{2,1,0:T(8,128)} %refs_2_.1, s32[2,2048]{1,0:T(2,128)} %refs_3_.1, s32[4,256]{1,0:T(4,128)} %refs_4_.1, ...), custom_call_target="tpu_custom_call" | custom-call | flops 17716740096 | bytes 33554432 | tf_op jit(solution)/shard_map/pallas_call | solution.py:1011
  152.0 0.0 copy-start
  152.0 0.0 copy-start.1
  152.0 0.0 copy-start.2
  152.0 4.9 %shard_map.103 = f32[1408,4,256]{2,1,0:T(4,128)} custom-call(bf16[4,1408,256]{2,1,0:T(8,128)(2,1)} %get-tuple-element.10.x), custom_call_target="tpu_custom_call" | custom-call | tf_op jit(solution)/shard_map/pallas_call | solution.py:1032
  156.9 0.0 copy-done
  156.9 1.6 %convert_element_type.6 = f32[4,256,512]{2,1,0:T(8,128)} convert(bf16[4,256,512]{2,1,0:T(8,128)(2,1)S(1)} %copy-done) | non-fusion elementwise | flops 524288 | bytes 3145728 | tf_op jit(solution)/shard_map/convert_element_type | solution.py:1040
  158.5 0.0 copy-done.1
  158.5 1.2 convert_element_type.7
  159.7 0.0 copy-done.2
  159.7 0.5 copy.12
Async XLA Ops:
  152.0 4.9 %copy-start = (bf16[4,256,512]{2,1,0:T(8,128)(2,1)S(1)}, bf16[4,256,512]{2,1,0:T(8,128)(2,1)}, u32[]{:S(2)}) copy-start(bf16[4,256,512]{2,1,0:T(8,128)(2,1)} %get-tuple-element.9) | copy-start | bytes 3145732
  152.0 6.5 %copy-start.1 = (bf16[1408,256]{1,0:T(8,128)(2,1)S(1)}, bf16[1408,256]{1,0:T(8,128)(2,1)}, u32[]{:S(2)}) copy-start(bf16[1408,256]{1,0:T(8,128)(2,1)} %get-tuple-element.11) | copy-start | bytes 2162692
  152.0 7.7 %copy-start.2 = (f32[2]{0:T(128)S(1)}, f32[2]{0:T(128)}, u32[]{:S(2)}) copy-start(f32[2]{0:T(128)} %get-tuple-element.16) | copy-start | bytes 28

commit v5 on v4

--- a/solution.py
+++ b/solution.py
@@ -624,59 +624,69 @@
 
     halves = (pl.ds(0, c_rows // 2), pl.ds(c_rows // 2, c_rows // 2))
 
-    def add_rows(dst, a, b):
+    def add_rows(dst, *terms):
         count = dst.shape[0] // 2
 
         def rows(i):
             at = pl.ds(pl.multiple_of(i * count, 8), count)
-            dst[at, :] = (a[at, :].astype(F32) + b[at, :].astype(F32)).astype(dst.dtype)
+            dst[at, :] = sum(t[at, :].astype(F32) for t in terms).astype(dst.dtype)
 
         loop(2, rows)
 
-    def scatter_0(k):
+    def multiply(k):
         mine, at, _ = place(k)
+        slot = rem(k, 2)
+        block = jnp.concatenate([dd[i, k].reshape(spots, LANES) for i in range(2)], axis=1)
+        out = jnp.dot(mm[...], block, preferred_element_type=F32).astype(BF16)
+        pss[slot, 0] = out[:, :LANES]
+        pss[slot, 1] = out[:, LANES:]
 
         @pl.when(jnp.logical_not(mine))
         def _():
-            for d in range(2):
-                remote(pss.at[rem(k, 2), d], rs1.at[d, at], o["r1_s"].at[d, at], o["r1_r"].at[d, at], mate).start()
+            for h, half in enumerate(halves):
+                for d in range(2):
+                    src, dst = pss.at[slot, d, half], rs1.at[d, at, half]
+                    remote(src, dst, o["r1_s"].at[d, at, h], o["r1_r"].at[d, at, h], mate).start()
 
     def stays(final):
         return sy_bit, jnp.where(final, sy_bit, 1 - sy_bit)
 
     def scatter_1(k):
         mine, at, final = place(k)
+        slot = rem(k, 2)
 
         @pl.when(mine)
         def _():
-            def each(d):
-                wait(rs1.at[d, at], o["r1_r"].at[d, at])
-                add_rows(rs1.at[d, at], pss.at[rem(k, 2), d], rs1.at[d, at])
-
-            loop(2, each)
-            for h, (d, to) in enumerate(zip(stays(final), (over_y, over_x), strict=True)):
-                src, dst = rs1.at[1 - d, at, halves[h]], rs2.at[at, halves[h]]
-                remote(src, dst, o["r2_s"].at[h, at], o["r2_r"].at[h, at], to).start()
+            for h, (stay, to) in enumerate(zip(stays(final), (over_y, over_x), strict=True)):
+                d, half = 1 - stay, halves[h]
+                src = rs1.at[d, at, half]
+                wait(src, o["r1_r"].at[d, at, h])
+                add_rows(src, pss.at[slot, d, half], src)
+                remote(src, rs2.at[at, half], o["r2_s"].at[h, at], o["r2_r"].at[h, at], to).start()
 
         @pl.when(jnp.logical_not(mine))
         def _():
             for d in range(2):
-                wait(pss.at[rem(k, 2), d], o["r1_s"].at[d, at])
+                for h, half in enumerate(halves):
+                    wait(pss.at[slot, d, half], o["r1_s"].at[d, at, h])
 
     def scatter_2(k):
         mine, at, final = place(k)
+        slot = rem(k, 2)
 
         @pl.when(mine)
         def _():
             i = rem(k, bpg)
             for h, (d, to) in enumerate(zip(stays(final), (over_x, over_y), strict=True)):
-                part = rs2.at[at, halves[h]]
+                half = halves[h]
+                part, first = rs2.at[at, half], rs1.at[d, at, half]
+                wait(first, o["r1_r"].at[d, at, h])
                 wait(part, o["r2_r"].at[h, at])
-                add_rows(part, rs1.at[d, at, halves[h]], part)
+                add_rows(part, pss.at[slot, d, half], first, part)
 
                 @pl.when(jnp.logical_not(final))
-                def _(h=h, part=part, to=to):
-                    remote(part, rs3.at[i, halves[h]], o["r3_s"].at[h, i], o["r3_r"].at[h, i], to).start()
+                def _(h=h, part=part, half=half, to=to):
+                    remote(part, rs3.at[i, half], o["r3_s"].at[h, i], o["r3_r"].at[h, i], to).start()
 
             for h, d in enumerate(stays(final)):
                 wait(rs1.at[1 - d, at, halves[h]], o["r2_s"].at[h, at])
@@ -706,12 +716,6 @@
         d = jnp.concatenate([dd[0, k, r], dd[1, k, r]], axis=1)
         new = lax.dot_general(x, d, (((1,), (1,)), ((), ())), preferred_element_type=F32)
         dm[r] = jnp.where(k == 0, 0.0, dm[r]) + new
-
-    def multiply(k, piece):
-        d = jnp.concatenate([dd[i, k].reshape(spots, LANES) for i in range(2)], axis=1)
-        out = jnp.dot(mm[...], d, preferred_element_type=F32).astype(BF16)
-        pss[rem(k, 2), 0] = out[:, :LANES]
-        pss[rem(k, 2), 1] = out[:, LANES:]
 
     def put_logits(r):
         return pltpu.make_async_copy(mm.at[:, r * width : (r + 1) * width], dlog.at[r], o["dl_m"].at[r])
@@ -866,8 +870,7 @@
         def _():
             @pl.when(piece == 0)
             def _():
-                multiply(k, piece)
-                scatter_0(k)
+                multiply(k)
 
         @pl.when((w >= 0) & (k == nb))
         def _():
@@ -990,8 +993,8 @@
         d_r=dma((2, nb, t_rows)),
         f_s=dma((2,)),
         f_r=dma((2,)),
-        r1_s=dma((2, nb // 2)),
-        r1_r=dma((2, nb // 2)),
+        r1_s=dma((2, nb // 2, 2)),
+        r1_r=dma((2, nb // 2, 2)),
         r2_s=dma((2, nb // 2)),
         r2_r=dma((2, nb // 2)),
         r3_s=dma((2, nb // 4)),

time: 160 us -> 160 us (level)
  no operation moved by 1% of the time
where the time goes in v5:
time: 160 us
  Pallas kernels  156 us (98%)
  other arithmetic  2.82 us (2%)
    pallas_call x1, Pallas kernels, per_device(): pl.pallas_call(functools.partial(kernel, names, sizes), out_shape=(jax.Sh...  151 us
    pallas_call x1, Pallas kernels, per_device(): pl.pallas_call(cells_first, grid=(c_rows // tile,), out_shape=jax.ShapeDt...  4.86 us

profile of v5, /device:TPU:1, one launch (start us, length us, event | category | flops | bytes accessed | tf_op | source)
XLA Modules:
  0.0 159.8 jit_solution(5551393618155206244)
XLA Ops:
  0.6 150.9 %shard_map.102 = (f32[2]{0:T(128)}, bf16[4,256,512]{2,1,0:T(8,128)(2,1)}, bf16[4,1408,256]{2,1,0:T(8,128)(2,1)}, bf16[1408,256]{1,0:T(8,128)(2,1)}) custom-call(f32[1408,4,256]{2,1,0:T(4,128)} %refs_0_.1, bf16[1408,2048]{1,0:T(8,128)(2,1)} %refs_1_.1, f32[4,256,2048]{2,1,0:T(8,128)} %refs_2_.1, s32[2,2048]{1,0:T(2,128)} %refs_3_.1, s32[4,256]{1,0:T(4,128)} %refs_4_.1, ...), custom_call_target="tpu_custom_call" | custom-call | flops 17716740096 | bytes 33554432 | tf_op jit(solution)/shard_map/pallas_call | solution.py:1014
  151.6 0.0 copy-start
  151.6 0.0 copy-start.1
  151.6 0.0 copy-start.2
  151.6 4.9 %shard_map.103 = f32[1408,4,256]{2,1,0:T(4,128)} custom-call(bf16[4,1408,256]{2,1,0:T(8,128)(2,1)} %get-tuple-element.10.x), custom_call_target="tpu_custom_call" | custom-call | tf_op jit(solution)/shard_map/pallas_call | solution.py:1035
  156.5 0.0 copy-done
  156.5 1.6 %convert_element_type.6 = f32[4,256,512]{2,1,0:T(8,128)} convert(bf16[4,256,512]{2,1,0:T(8,128)(2,1)S(1)} %copy-done) | non-fusion elementwise | flops 524288 | bytes 3145728 | tf_op jit(solution)/shard_map/convert_element_type | solution.py:1043
  158.1 0.0 copy-done.1
  158.1 1.2 convert_element_type.7
  159.3 0.0 copy-done.2
  159.3 0.5 copy.12
Async XLA Ops:
  151.6 4.9 %copy-start = (bf16[4,256,512]{2,1,0:T(8,128)(2,1)S(1)}, bf16[4,256,512]{2,1,0:T(8,128)(2,1)}, u32[]{:S(2)}) copy-start(bf16[4,256,512]{2,1,0:T(8,128)(2,1)} %get-tuple-element.9) | copy-start | bytes 3145732
  151.6 6.5 %copy-start.1 = (bf16[1408,256]{1,0:T(8,128)(2,1)S(1)}, bf16[1408,256]{1,0:T(8,128)(2,1)}, u32[]{:S(2)}) copy-start(bf16[1408,256]{1,0:T(8,128)(2,1)} %get-tuple-element.11) | copy-start | bytes 2162692
  151.6 7.7 %copy-start.2 = (f32[2]{0:T(128)S(1)}, f32[2]{0:T(128)}, u32[]{:S(2)}) copy-start(f32[2]{0:T(128)} %get-tuple-element.16) | copy-start | bytes 28

commit v6 on v5

--- a/solution.py
+++ b/solution.py
@@ -63,7 +63,7 @@
     bpg = nb // 4
     tile = LANES
     tiles = c_rows // tile
-    quarter = c_rows // t_rows
+    quarter = c_rows // 4
     sub = min(64, width)
     mid = slice(8, 8 + width)
 
@@ -350,7 +350,7 @@
 
         loop(n // 2 - 1, each)
 
-    early_pred = 1 if n == 4 else 0
+    early_pred = 2 if n == 4 else 0
 
     def plane_peer(j):
         t = rem(here + j + 1, nplane)
@@ -422,7 +422,8 @@
                 def _():
                     predict(d, div(k, 2) + 1, r)
 
-        loop(2, direction)
+        turn = cz - 1 > n - 2 - cz
+        loop(2, lambda i: direction(jnp.where(turn, 1 - i, i)))
 
         @pl.when(owner & (s == half * t_rows))
         def _():
@@ -623,6 +624,7 @@
         return rem(jj, 2) == sy, hi * bpg + rem(k, bpg), jnp.where(sy_bit == 0, 1 - hi, hi) == sx_bit
 
     halves = (pl.ds(0, c_rows // 2), pl.ds(c_rows // 2, c_rows // 2))
+    cuts = [pl.ds(i * quarter, quarter) for i in range(4)]
 
     def add_rows(dst, *terms):
         count = dst.shape[0] // 2
@@ -659,10 +661,11 @@
         def _():
             for h, (stay, to) in enumerate(zip(stays(final), (over_y, over_x), strict=True)):
                 d, half = 1 - stay, halves[h]
-                src = rs1.at[d, at, half]
-                wait(src, o["r1_r"].at[d, at, h])
-                add_rows(src, pss.at[slot, d, half], src)
-                remote(src, rs2.at[at, half], o["r2_s"].at[h, at], o["r2_r"].at[h, at], to).start()
+                wait(rs1.at[d, at, half], o["r1_r"].at[d, at, h])
+                for i in (2 * h, 2 * h + 1):
+                    src, sems = rs1.at[d, at, cuts[i]], (o["r2_s"].at[i, at], o["r2_r"].at[i, at])
+                    add_rows(src, pss.at[slot, d, cuts[i]], src)
+                    remote(src, rs2.at[at, cuts[i]], *sems, to).start()
 
         @pl.when(jnp.logical_not(mine))
         def _():
@@ -676,20 +679,22 @@
 
         @pl.when(mine)
         def _():
-            i = rem(k, bpg)
-            for h, (d, to) in enumerate(zip(stays(final), (over_x, over_y), strict=True)):
-                half = halves[h]
-                part, first = rs2.at[at, half], rs1.at[d, at, half]
-                wait(first, o["r1_r"].at[d, at, h])
-                wait(part, o["r2_r"].at[h, at])
-                add_rows(part, pss.at[slot, d, half], first, part)
+            j = rem(k, bpg)
+            for h, d in enumerate(stays(final)):
+                wait(rs1.at[d, at, halves[h]], o["r1_r"].at[d, at, h])
+            for i in (0, 2, 1, 3):
+                h, cut = i // 2, cuts[i]
+                d, to = stays(final)[h], (over_x, over_y)[h]
+                part = rs2.at[at, cut]
+                wait(part, o["r2_r"].at[i, at])
+                add_rows(part, pss.at[slot, d, cut], rs1.at[d, at, cut], part)
 
                 @pl.when(jnp.logical_not(final))
-                def _(h=h, part=part, half=half, to=to):
-                    remote(part, rs3.at[i, half], o["r3_s"].at[h, i], o["r3_r"].at[h, i], to).start()
-
-            for h, d in enumerate(stays(final)):
-                wait(rs1.at[1 - d, at, halves[h]], o["r2_s"].at[h, at])
+                def _(i=i, part=part, cut=cut, to=to):
+                    remote(part, rs3.at[j, cut], o["r3_s"].at[i, j], o["r3_r"].at[i, j], to).start()
+
+            for i in range(4):
+                wait(rs1.at[1 - stays(final)[i // 2], at, cuts[i]], o["r2_s"].at[i, at])
 
     def put_cells(i):
         at = pl.ds(pl.multiple_of(i * LANES, LANES), LANES)
@@ -701,15 +706,15 @@
 
         @pl.when(mine & final)
         def _():
-            for h in range(2):
-                wait(rs3.at[i, halves[h]], o["r3_r"].at[h, i])
-                add_rows(dcv.at[i, halves[h]], rs2.at[at, halves[h]], rs3.at[i, halves[h]])
+            for c in (0, 2, 1, 3):
+                wait(rs3.at[i, cuts[c]], o["r3_r"].at[c, i])
+                add_rows(dcv.at[i, cuts[c]], rs2.at[at, cuts[c]], rs3.at[i, cuts[c]])
             put_cells(i).start()
 
         @pl.when(mine & jnp.logical_not(final))
         def _():
-            for h in range(2):
-                wait(rs2.at[at, halves[h]], o["r3_s"].at[h, i])
+            for c in range(4):
+                wait(rs2.at[at, cuts[c]], o["r3_s"].at[c, i])
 
     def add_map(k, r):
         x = jnp.concatenate([xs[gene_block(0, k)], xs[gene_block(1, k)]], axis=1)
@@ -856,21 +861,20 @@
                 def _():
                     remote(fm.at[d], fm.at[d], o["f_s"].at[d], o["f_r"].at[d], to).start()
 
-        loop(2, direction)
+        turn = cz - 1 < n - 2 - cz
+        loop(2, lambda i: direction(jnp.where(turn, 1 - i, i)))
         q = s - lag
 
+        w = q - t_rows + 1
+        k, piece = div(w, t_rows), rem(w, t_rows)
+
+        @pl.when((w >= 0) & (k < nb) & (piece == 0))
+        def _():
+            multiply(k)
+
         @pl.when((q >= 0) & (q < nb * t_rows))
         def _():
             add_map(*back_chunk(q))
-
-        w = q - t_rows
-        k, piece = div(w, t_rows), rem(w, t_rows)
-
-        @pl.when((w >= 0) & (k < nb))
-        def _():
-            @pl.when(piece == 0)
-            def _():
-                multiply(k)
 
         @pl.when((w >= 0) & (k == nb))
         def _():
@@ -995,10 +999,10 @@
         f_r=dma((2,)),
         r1_s=dma((2, nb // 2, 2)),
         r1_r=dma((2, nb // 2, 2)),
-        r2_s=dma((2, nb // 2)),
-        r2_r=dma((2, nb // 2)),
-        r3_s=dma((2, nb // 4)),
-        r3_r=dma((2, nb // 4)),
+        r2_s=dma((4, nb // 2)),
+        r2_r=dma((4, nb // 2)),
+        r3_s=dma((4, nb // 4)),
+        r3_r=dma((4, nb // 4)),
         gp_s=dma((max(n // 2 - 1, 1), wb)),
         gp_r=dma((wb,)),
         gq_s=dma((max(n // 2 - 1, 1), wb)),

time: 160 us -> 159 us (level)
  no operation moved by 1% of the time
where the time goes in v6:
time: 159 us
  Pallas kernels  155 us (97%)
  other arithmetic  2.82 us (2%)
    pallas_call x1, Pallas kernels, per_device(): pl.pallas_call(functools.partial(kernel, names, sizes), out_shape=(jax.Sh...  150 us
    pallas_call x1, Pallas kernels, per_device(): pl.pallas_call(cells_first, grid=(c_rows // tile,), out_shape=jax.ShapeDt...  4.86 us

profile of v6, /device:TPU:1, one launch (start us, length us, event | category | flops | bytes accessed | tf_op | source)
XLA Modules:
  0.0 159.0 jit_solution(4578065308737266003)
XLA Ops:
  0.6 150.1 %shard_map.102 = (f32[2]{0:T(128)}, bf16[4,256,512]{2,1,0:T(8,128)(2,1)}, bf16[4,1408,256]{2,1,0:T(8,128)(2,1)}, bf16[1408,256]{1,0:T(8,128)(2,1)}) custom-call(f32[1408,4,256]{2,1,0:T(4,128)} %refs_0_.1, bf16[1408,2048]{1,0:T(8,128)(2,1)} %refs_1_.1, f32[4,256,2048]{2,1,0:T(8,128)} %refs_2_.1, s32[2,2048]{1,0:T(2,128)} %refs_3_.1, s32[4,256]{1,0:T(4,128)} %refs_4_.1, ...), custom_call_target="tpu_custom_call" | custom-call | flops 17716740096 | bytes 33554432 | tf_op jit(solution)/shard_map/pallas_call | solution.py:1018
  150.8 0.0 copy-start
  150.8 0.0 copy-start.1
  150.8 0.0 copy-start.2
  150.8 4.9 %shard_map.103 = f32[1408,4,256]{2,1,0:T(4,128)} custom-call(bf16[4,1408,256]{2,1,0:T(8,128)(2,1)} %get-tuple-element.10.x), custom_call_target="tpu_custom_call" | custom-call | tf_op jit(solution)/shard_map/pallas_call | solution.py:1039
  155.7 0.0 copy-done
  155.7 1.6 %convert_element_type.6 = f32[4,256,512]{2,1,0:T(8,128)} convert(bf16[4,256,512]{2,1,0:T(8,128)(2,1)S(1)} %copy-done) | non-fusion elementwise | flops 524288 | bytes 3145728 | tf_op jit(solution)/shard_map/convert_element_type | solution.py:1047
  157.3 0.0 copy-done.1
  157.3 1.2 convert_element_type.7
  158.5 0.0 copy-done.2
  158.5 0.5 copy.12
Async XLA Ops:
  150.8 4.9 %copy-start = (bf16[4,256,512]{2,1,0:T(8,128)(2,1)S(1)}, bf16[4,256,512]{2,1,0:T(8,128)(2,1)}, u32[]{:S(2)}) copy-start(bf16[4,256,512]{2,1,0:T(8,128)(2,1)} %get-tuple-element.9) | copy-start | bytes 3145732
  150.8 6.5 %copy-start.1 = (bf16[1408,256]{1,0:T(8,128)(2,1)S(1)}, bf16[1408,256]{1,0:T(8,128)(2,1)}, u32[]{:S(2)}) copy-start(bf16[1408,256]{1,0:T(8,128)(2,1)} %get-tuple-element.11) | copy-start | bytes 2162692
  150.8 7.7 %copy-start.2 = (f32[2]{0:T(128)S(1)}, f32[2]{0:T(128)}, u32[]{:S(2)}) copy-start(f32[2]{0:T(128)} %get-tuple-element.16) | copy-start | bytes 28

commit v7 on v6

--- a/solution.py
+++ b/solution.py
@@ -635,20 +635,20 @@
 
         loop(2, rows)
 
-    def multiply(k):
+    def multiply(k, h):
+        half = halves[h]
         mine, at, _ = place(k)
         slot = rem(k, 2)
         block = jnp.concatenate([dd[i, k].reshape(spots, LANES) for i in range(2)], axis=1)
-        out = jnp.dot(mm[...], block, preferred_element_type=F32).astype(BF16)
-        pss[slot, 0] = out[:, :LANES]
-        pss[slot, 1] = out[:, LANES:]
+        out = jnp.dot(mm[half, :], block, preferred_element_type=F32).astype(BF16)
+        pss[slot, 0, half, :] = out[:, :LANES]
+        pss[slot, 1, half, :] = out[:, LANES:]
 
         @pl.when(jnp.logical_not(mine))
         def _():
-            for h, half in enumerate(halves):
-                for d in range(2):
-                    src, dst = pss.at[slot, d, half], rs1.at[d, at, half]
-                    remote(src, dst, o["r1_s"].at[d, at, h], o["r1_r"].at[d, at, h], mate).start()
+            for d in range(2):
+                src, dst = pss.at[slot, d, half], rs1.at[d, at, half]
+                remote(src, dst, o["r1_s"].at[d, at, h], o["r1_r"].at[d, at, h], mate).start()
 
     def stays(final):
         return sy_bit, jnp.where(final, sy_bit, 1 - sy_bit)
@@ -868,9 +868,10 @@
         w = q - t_rows + 1
         k, piece = div(w, t_rows), rem(w, t_rows)
 
-        @pl.when((w >= 0) & (k < nb) & (piece == 0))
-        def _():
-            multiply(k)
+        for h in range(2):
+            @pl.when((w >= 0) & (k < nb) & (piece == h))
+            def _(h=h):
+                multiply(k, h)
 
         @pl.when((q >= 0) & (q < nb * t_rows))
         def _():

time: 159 us -> 159 us (level)
  no operation moved by 1% of the time
where the time goes in v7:
time: 159 us
  Pallas kernels  155 us (97%)
  other arithmetic  2.82 us (2%)
    pallas_call x1, Pallas kernels, per_device(): pl.pallas_call(functools.partial(kernel, names, sizes), out_shape=(jax.Sh...  150 us
    pallas_call x1, Pallas kernels, per_device(): pl.pallas_call(cells_first, grid=(c_rows // tile,), out_shape=jax.ShapeDt...  4.86 us

profile of v7, /device:TPU:1, one launch (start us, length us, event | category | flops | bytes accessed | tf_op | source)
XLA Modules:
  0.0 158.9 jit_solution(5624490463317402934)
XLA Ops:
  0.6 150.1 %shard_map.102 = (f32[2]{0:T(128)}, bf16[4,256,512]{2,1,0:T(8,128)(2,1)}, bf16[4,1408,256]{2,1,0:T(8,128)(2,1)}, bf16[1408,256]{1,0:T(8,128)(2,1)}) custom-call(f32[1408,4,256]{2,1,0:T(4,128)} %refs_0_.1, bf16[1408,2048]{1,0:T(8,128)(2,1)} %refs_1_.1, f32[4,256,2048]{2,1,0:T(8,128)} %refs_2_.1, s32[2,2048]{1,0:T(2,128)} %refs_3_.1, s32[4,256]{1,0:T(4,128)} %refs_4_.1, ...), custom_call_target="tpu_custom_call" | custom-call | flops 17716740096 | bytes 33554432 | tf_op jit(solution)/shard_map/pallas_call | solution.py:1019
  150.7 0.0 copy-start
  150.7 0.0 copy-start.1
  150.7 0.0 copy-start.2
  150.7 4.9 %shard_map.103 = f32[1408,4,256]{2,1,0:T(4,128)} custom-call(bf16[4,1408,256]{2,1,0:T(8,128)(2,1)} %get-tuple-element.10.x), custom_call_target="tpu_custom_call" | custom-call | tf_op jit(solution)/shard_map/pallas_call | solution.py:1040
  155.6 0.0 copy-done
  155.6 1.6 %convert_element_type.6 = f32[4,256,512]{2,1,0:T(8,128)} convert(bf16[4,256,512]{2,1,0:T(8,128)(2,1)S(1)} %copy-done) | non-fusion elementwise | flops 524288 | bytes 3145728 | tf_op jit(solution)/shard_map/convert_element_type | solution.py:1048
  157.2 0.0 copy-done.1
  157.2 1.2 convert_element_type.7
  158.4 0.0 copy-done.2
  158.4 0.5 copy.12
Async XLA Ops:
  150.7 4.9 %copy-start = (bf16[4,256,512]{2,1,0:T(8,128)(2,1)S(1)}, bf16[4,256,512]{2,1,0:T(8,128)(2,1)}, u32[]{:S(2)}) copy-start(bf16[4,256,512]{2,1,0:T(8,128)(2,1)} %get-tuple-element.9) | copy-start | bytes 3145732
  150.7 6.5 %copy-start.1 = (bf16[1408,256]{1,0:T(8,128)(2,1)S(1)}, bf16[1408,256]{1,0:T(8,128)(2,1)}, u32[]{:S(2)}) copy-start(bf16[1408,256]{1,0:T(8,128)(2,1)} %get-tuple-element.11) | copy-start | bytes 2162692
  150.7 7.7 %copy-start.2 = (f32[2]{0:T(128)S(1)}, f32[2]{0:T(128)}, u32[]{:S(2)}) copy-start(f32[2]{0:T(128)} %get-tuple-element.16) | copy-start | bytes 28
